TPU v7x, 512 devices: a whole 4x4x16 slice. The times are simulated.
512 devices in a mesh: dp: 16 (over z), fsdp: 32 (over y, x, core).
Axes of the slice: x: 4, y: 4, z: 16, core: 2. Of those that a mesh axis runs over, the one named last changes fastest.
Arguments:
- features: bfloat16 [32768, 8192], P('dp', 'fsdp'), may hold values from -6 to 6
- out_cotangent: bfloat16 [32768, 8192], P('dp', 'fsdp'), may hold values from -0.3125 to 0.3125
- head_cotangents: bfloat16 [32768, 1280], P(('dp', 'fsdp')), may hold values from -0.3125 to 0.3125
- attention_out: bfloat16 [32768, 1024], P(('dp', 'fsdp')), may hold values from -6 to 6
- momentum: float32 [18, 8192, 128], P(None, 'fsdp'), may hold values from -6 to 6
- lengths: int32 [16], P('dp'), may hold values from 1 to 2048
Outputs:
- updates: bfloat16 [18, 8192, 128], P(None, 'fsdp')
All inputs are finite; a program needn't handle non-finite values.
Results may differ from a plain program's by a relative error of at most 0.0052.
Values may be sent and summed in bfloat16 or wider, within the bound.
No kernel may reach another device: no remote copies, remote signals or barrier semaphores. Data moves between devices by JAX's collectives and lax.ppermute only.
A program may use at most 64 MiB of HBM per device.

v0:
```python
import math

import jax
import jax.numpy as jnp
from jax import lax
from jax.sharding import PartitionSpec as P

ITERS = 3


coef_a = 3.4445
coef_b = -4.775
coef_c = 2.0315
momentum_decay = 0.95
update_gain = 0.2
norm_floor = 1e-07


def poly_step(iterate, gram_sum):
    highest = lax.Precision.HIGHEST
    poly_term = coef_b * gram_sum + coef_c * jnp.einsum(
        "mcd,mde->mce", gram_sum, gram_sum, precision=highest
    )
    return coef_a * iterate + jnp.einsum("mrc,mcd->mrd", iterate, poly_term, precision=highest)


def nesterov_blend(gradient, moment_rows):
    new_moment = momentum_decay * moment_rows + gradient
    return (gradient + momentum_decay * new_moment).astype(jnp.bfloat16)


def whole_orthogonal(received, out_scale):
    highest = lax.Precision.HIGHEST
    matrices = received[:, 0].astype(jnp.float32)
    sum_squares = jnp.sum(matrices * matrices, axis=(1, 2))
    iterate = matrices / (jnp.sqrt(sum_squares) + norm_floor)[:, None, None]
    for iteration in range(ITERS):
        gram_sum = jnp.einsum("mrc,mrd->mcd", iterate, iterate, precision=highest)
        iterate = poly_step(iterate, gram_sum)
    return (out_scale * iterate).astype(jnp.bfloat16)[:, None]


def local(features, out_cotangent, head_cotangents, attention_out, momentum, lengths):
    tok_count, row_count = features.shape
    mat_count, head_size = (momentum.shape[0], momentum.shape[2])
    seq_count = lengths.shape[0]
    slot_len = tok_count // seq_count
    positions = lax.iota(jnp.int32, tok_count)
    owner_seq = (positions // slot_len)[:, None] == lax.iota(jnp.int32, seq_count)[None, :]
    limits = jnp.sum(jnp.where(owner_seq, lengths[None, :], 0), axis=1)
    live_mask = (positions % slot_len < limits).astype(jnp.bfloat16)[:, None]
    local_in = features * live_mask
    local_out = out_cotangent * live_mask
    contract = (((0,), (0,)), ((), ()))
    part_in = lax.dot_general(
        local_in,
        lax.all_gather(head_cotangents, "fsdp", axis=0, tiled=True),
        contract,
        preferred_element_type=jnp.float32,
    )
    part_out = lax.dot_general(
        local_out,
        lax.all_gather(attention_out, "fsdp", axis=0, tiled=True),
        contract,
        preferred_element_type=jnp.float32,
    )
    gradient = (
        jnp.concatenate([part_in, part_out], axis=1)
        .reshape(row_count, mat_count, head_size)
        .transpose(1, 0, 2)
    )
    full_rows = row_count * lax.axis_size("fsdp")
    out_scale = update_gain * math.sqrt(max(full_rows, head_size))
    owner_count = lax.axis_size("fsdp")
    summed = lax.psum(gradient, "dp")
    blended = nesterov_blend(summed, momentum)
    slot_count = (mat_count + owner_count - 1) // owner_count
    padded = slot_count * owner_count
    send_buffer = jnp.pad(blended, ((0, padded - mat_count), (0, 0), (0, 0))).reshape(
        slot_count, owner_count, row_count, head_size
    )
    result = whole_orthogonal(
        lax.all_to_all(send_buffer, "fsdp", split_axis=1, concat_axis=2, tiled=True), out_scale
    )
    returned = lax.all_to_all(result, "fsdp", split_axis=2, concat_axis=1, tiled=True)
    updates = returned.reshape(padded, row_count, head_size)[:mat_count]
    return updates


def solution(mesh):
    return jax.shard_map(
        local,
        mesh=mesh,
        in_specs=(
            P("dp", "fsdp"),
            P("dp", "fsdp"),
            P(("dp", "fsdp"), None),
            P(("dp", "fsdp"), None),
            P(None, "fsdp", None),
            P("dp"),
        ),
        out_specs=P(None, "fsdp", None),
        check_vma=False,
    )
```

profile of v0, /device:TPU:1, one launch (start us, length us, event | category | flops | bytes accessed | tf_op | source)
XLA Modules:
  0.0 501.7 jit_solution(14042845324500913415)
XLA Ops:
  6.5 0.7 all-gather.5.cloned.1.call-update
  7.3 0.7 all-gather.3.cloned.1.call-update
  8.7 68.9 %all-gather.5.cloned.1.call-done = bf16[2048,1024]{1,0:T(8,128)(2,1)} async-done(((bf16[64,1024]{1,0:T(8,128)(2,1)}), bf16[2048,1024]{1,0:T(8,128)(2,1)}) %all-gather.5.cloned.1.call-update) | async-done | bytes 4194320 | tf_op jit(solution)/shard_map/all_gather | solution.py:63
  77.6 3.9 fusion.12
  81.5 61.5 %all-gather.3.cloned.1.call-done = bf16[2048,1280]{1,0:T(8,128)(2,1)} async-done(((bf16[64,1280]{1,0:T(8,128)(2,1)}), bf16[2048,1280]{1,0:T(8,128)(2,1)}) %all-gather.3.cloned.1.call-update) | async-done | bytes 5242896 | tf_op jit(solution)/shard_map/all_gather | solution.py:57
  143.1 4.2 fusion.14
  147.4 1.9 copy.18
  149.4 2.0 copy.19
  151.4 134.0 %all-reduce.3.cloned.1.call-done = f32[18,256,128]{1,2,0:T(8,128)} async-done(((f32[18,256,128]{1,2,0:T(8,128)}), f32[18,256,128]{1,2,0:T(8,128)}) %all-reduce.3.cloned.1.call-update) | async-done | bytes 2359312 | tf_op jit(solution)/shard_map/psum | solution.py:75
  285.4 2.1 add_convert_fusion
  287.5 0.2 pad_bitcast_fusion
  287.7 2.9 copy.20
  290.6 45.0 %all_to_all.21 = bf16[1,32,256,128]{3,2,0,1:T(8,128)(2,1)S(1)} all-to-all(bf16[1,32,256,128]{3,2,0,1:T(8,128)(2,1)} %copy.20), channel_id=1, replica_groups=mesh['dp'=16,'fsdp'=32] {'fsdp'}, dimensions={1} | all-to-all | bytes 4194304 | tf_op jit(solution)/shard_map/all_to_all | solution.py:83
  335.6 1.7 fusion.3
  337.9 7.2 %fusion.6 = f32[128,128]{1,0:T(8,128)S(1)} fusion(bf16[1,32,256,128]{3,2,0,1:T(8,128)(2,1)S(1)} %all_to_all.21, f32[]{:T(128)S(6)} %add.58), kind=kOutput, calls=%fused_computation.15 | convolution fusion | flops 1612709888 | bytes 2162692 | tf_op jit(solution)/shard_map/mrc,mrd->mcd/dot_general | solution.py:38
  345.2 0.2 fusion.11
  345.4 0.5 convert_divide_fusion
  345.9 3.6 convolution_add_fusion.2
  349.6 6.7 %fusion.26 = f32[128,128]{1,0:T(8,128)S(1)} fusion(f32[8192,128]{1,0:T(8,128)S(1)} %convolution_add_fusion.2), kind=kOutput, calls=%fused_computation.42 | convolution fusion | flops 1610612736 | bytes 4259840 | tf_op jit(solution)/shard_map/mrc,mrd->mcd/dot_general | solution.py:38
  356.3 0.2 fusion.10
  356.5 3.4 convolution_add_fusion.1
  359.9 7.1 %fusion.27 = f32[128,128]{1,0:T(8,128)S(1)} fusion(f32[8192,128]{1,0:T(8,128)S(1)} %convolution_add_fusion.1), kind=kOutput, calls=%fused_computation.43 | convolution fusion | flops 1610612736 | bytes 4259840 | tf_op jit(solution)/shard_map/mrc,mrd->mcd/dot_general | solution.py:38
  367.1 0.2 fusion.9
  367.3 3.6 fusion.2
  370.9 33.4 %copy.27 = bf16[1,1,8192,128]{3,1,0,2:T(2,128)(2,1)} copy(bf16[1,1,8192,128]{3,2,1,0:T(8,128)(2,1)S(1)} %fusion.2) | data formatting | bytes 4194304 | tf_op jit(solution)/shard_map/broadcast_in_dim | solution.py:40
  404.4 0.5 broadcast.141
  404.9 45.2 %reduce.3 = bf16[8192,128]{1,0:T(8,128)(2,1)S(1)} reduce(bf16[8192,1,1,128]{3,2,1,0:T(2,128)(2,1)} %bitcast.48, bf16[]{:T(256)} %broadcast.141), dimensions={1,2}, to_apply=%bitcast.46.reduce_sub_computation | reduce | bytes 4194306
  450.1 2.1 reshape.144
  452.1 32.6 %all_to_all.22 = bf16[32,2,16384]{2,1,0:T(2,128)(2,1)S(1)} all-to-all(bf16[32,2,16384]{2,1,0:T(2,128)(2,1)} %reshape.144), channel_id=1, replica_groups=mesh['dp'=16,'fsdp'=32] {'fsdp'}, dimensions={0} | all-to-all | bytes 4194304 | tf_op jit(solution)/shard_map/all_to_all | solution.py:85
  484.7 6.8 %reshape.145 = bf16[8192,1,1,128]{3,2,1,0:T(2,128)(2,1)} reshape(bf16[32,2,16384]{2,1,0:T(2,128)(2,1)S(1)} %all_to_all.22) | data formatting | bytes 4194304
  491.5 2.5 copy.25
  493.9 1.1 slice_bitcast_fusion
  (8 shorter events, 0.3 us)
Async XLA Ops:
  6.5 136.5 %copy-start = (bf16[2048,256]{1,0:T(8,128)(2,1)S(1)}, bf16[2048,256]{1,0:T(8,128)(2,1)}, u32[]{:S(2)}) copy-start(bf16[2048,256]{1,0:T(8,128)(2,1)} %param.6) | copy-start | bytes 3145732
  6.5 71.1 %all-gather.5.cloned.1.call-start = ((), (), s32[]{:S(2)}) async-start(), calls=%async_computation.3 | async-start | bytes 4325376 | tf_op jit(solution)/shard_map/all_gather | solution.py:63
  7.3 135.8 %all-gather.3.cloned.1.call-start = ((), (), s32[]{:S(2)}) async-start(), calls=%async_computation.2 | async-start | bytes 5406720 | tf_op jit(solution)/shard_map/all_gather | solution.py:57
  8.0 277.4 %all-reduce.3.cloned.1.call-start = ((), (), s32[]{:S(2)}) async-start(), calls=%async_computation.4 | async-start | bytes 4718592 | tf_op jit(solution)/shard_map/psum | solution.py:75
Sparse Core Ops, SparseCore 0:
  10.5 67.0 all-gather.4
  80.8 62.2 all-gather.2
  149.5 135.8 all-reduce.2
where the time goes:
time: 506 us; the launch traced here: 502 us
  waiting for transfers between devices  266 us (53%)
  blocking collectives  77.5 us (15%)
  local copies, waits for them, and re-layouts  53.4 us (11%)
  other arithmetic  49.7 us (10%)
  matrix products  40.5 us (8%)
  between operations  14.8 us (3%)
    psum x1, waiting for transfers between devices, local(): summed = lax.psum(gradient, 'dp')  134 us
    all_gather x1, waiting for transfers between devices, local(): lax.all_gather(attention_out, 'fsdp', axis=0, tiled=True)  68.9 us
    all_gather x1, waiting for transfers between devices, local(): lax.all_gather(head_cotangents, 'fsdp', axis=0, tiled=True)  61.5 us
    unnamed x1, other arithmetic  45.2 us
    all_to_all x1, blocking collectives, local(): lax.all_to_all(send_buffer, 'fsdp', split_axis=1, concat_axis=2, tiled=True)  45 us
    broadcast_in_dim x1, local copies, waits for them, and re-layouts, whole_orthogonal(): return (out_scale * iterate).astype(jnp.bfloat16)[:, None]  33.4 us
    all_to_all x1, blocking collectives, local(): lax.all_to_all(result, 'fsdp', split_axis=2, concat_axis=1, tiled=True)  32.6 us
    dot_general x3, matrix products, whole_orthogonal(): gram_sum = jnp.einsum('mrc,mrd->mcd', iterate, iterate, precision=highest)  21.1 us
  transfers between devices with their start and end apart: 3, of which 3 were waited for; matrix products, arithmetic and copies ran while one was open for 1% of the time, Pallas kernels for 0%

commit v1 on v0

v1 whole, which is shorter than its diff:
```python
import math

import jax
import jax.numpy as jnp
from jax import lax
from jax.sharding import PartitionSpec as P

ITERS = 3


coef_a = 3.4445
coef_b = -4.775
coef_c = 2.0315
momentum_decay = 0.95
update_gain = 0.2
norm_floor = 1e-07


def nesterov_blend(gradient, moment_rows):
    new_moment = momentum_decay * moment_rows + gradient
    return (gradient + momentum_decay * new_moment).astype(jnp.bfloat16)


def poly_of_gram(gram, out_scale):
    highest = lax.Precision.HIGHEST

    def mul(left, right):
        return jnp.einsum("mij,mjk->mik", left, right, precision=highest)

    size = gram.shape[-1]
    eye = jnp.eye(size, dtype=jnp.float32)[None]
    sum_squares = jnp.sum(gram * eye, axis=(1, 2), keepdims=True)
    inverse = 1.0 / (jnp.sqrt(sum_squares) + norm_floor)
    current = gram * inverse * inverse
    factor = eye * (inverse * out_scale)
    for iteration in range(ITERS):
        step = coef_a * eye + coef_b * current + coef_c * mul(current, current)
        factor = mul(factor, step) if iteration else factor[:, :1, :1] * step
        if iteration < ITERS - 1:
            current = mul(mul(current, step), step)
    return factor


def split_product(rows, factor):
    high = factor.astype(jnp.bfloat16)
    low = (factor - high.astype(jnp.float32)).astype(jnp.bfloat16)
    product = jnp.dot(rows, high, preferred_element_type=jnp.float32)
    product += jnp.dot(rows, low, preferred_element_type=jnp.float32)
    return product.astype(jnp.bfloat16)


def local(features, out_cotangent, head_cotangents, attention_out, momentum, lengths):
    tok_count, row_count = features.shape
    mat_count, _, head_size = momentum.shape
    groups, owners = lax.axis_size("dp"), lax.axis_size("fsdp")
    in_width = head_cotangents.shape[1]
    group = lax.axis_index("dp")
    extra = mat_count - groups
    share = extra * row_count // groups
    per_extra = groups // extra

    live = lax.iota(jnp.int32, tok_count) < lengths[0]
    live_mask = live.astype(jnp.bfloat16)[:, None]
    heads = lax.all_gather(
        jnp.concatenate([head_cotangents, attention_out], axis=1), "fsdp", axis=0, tiled=True
    )
    contract = (((0,), (0,)), ((), ()))
    part_in = lax.dot_general(
        features * live_mask, heads[:, :in_width], contract, preferred_element_type=jnp.float32
    )
    part_out = lax.dot_general(
        out_cotangent * live_mask, heads[:, in_width:], contract, preferred_element_type=jnp.float32
    )
    partial = jnp.concatenate([part_in, part_out], axis=1).astype(jnp.bfloat16)
    partial = partial.reshape(row_count, mat_count, head_size).transpose(1, 0, 2)
    partial = jnp.concatenate(
        [partial[:groups], partial[groups:].reshape(groups, share, head_size)], axis=1
    )
    received = lax.all_to_all(partial, "dp", 0, 0, tiled=True)
    gradient = jnp.sum(received.astype(jnp.float32), axis=0)
    moment_main = lax.dynamic_index_in_dim(momentum, group, 0, keepdims=False)
    moment_rest = lax.dynamic_index_in_dim(
        momentum[groups:].reshape(groups, share, head_size), group, 0, keepdims=False
    )
    main = nesterov_blend(gradient[:row_count], moment_main)
    rest = nesterov_blend(gradient[row_count:], moment_rest)

    gram_main = lax.dot_general(main, main, contract, preferred_element_type=jnp.float32)
    gram_rest = lax.dot_general(rest, rest, contract, preferred_element_type=jnp.float32)
    slab = head_size // owners
    both = jnp.concatenate(
        [gram_main.reshape(owners, slab, head_size), gram_rest.reshape(owners, slab, head_size)], axis=1
    )
    summed = jnp.sum(lax.all_to_all(both, "fsdp", 0, 0, tiled=True), axis=0)
    octets = [[e * per_extra + i for i in range(per_extra)] for e in range(extra)]
    rest_sum = jnp.sum(
        lax.all_to_all(
            jnp.broadcast_to(summed[None, slab:], (per_extra, slab, head_size)),
            "dp", 0, 0, axis_index_groups=octets, tiled=True,
        ),
        axis=0,
    )
    summed = jnp.concatenate([summed[:slab], rest_sum], axis=0)
    grams = lax.all_to_all(
        jnp.broadcast_to(summed[None], (owners, 2 * slab, head_size)), "fsdp", 0, 0, tiled=True
    )
    grams = grams.reshape(owners, 2, slab, head_size).transpose(1, 0, 2, 3)
    out_scale = update_gain * math.sqrt(max(row_count * owners, head_size))
    factors = poly_of_gram(grams.reshape(2, head_size, head_size), out_scale)
    update_main = split_product(main, factors[0])
    update_rest = split_product(rest, factors[1])

    cut = row_count - share
    first = lax.all_gather(update_main[:cut], "dp", axis=0)
    tail = jnp.concatenate([update_main[cut:], update_rest], axis=0)
    second = lax.all_to_all(
        jnp.broadcast_to(tail[None], (groups,) + tail.shape), "dp", 0, 0, tiled=True
    )
    mains = jnp.concatenate([first, second[:, :share]], axis=1)
    rests = second[:, share:].reshape(extra, row_count, head_size)
    return jnp.concatenate([mains, rests], axis=0)


def solution(mesh):
    return jax.shard_map(
        local,
        mesh=mesh,
        in_specs=(
            P("dp", "fsdp"),
            P("dp", "fsdp"),
            P(("dp", "fsdp"), None),
            P(("dp", "fsdp"), None),
            P(None, "fsdp", None),
            P("dp"),
        ),
        out_specs=P(None, "fsdp", None),
        check_vma=False,
    )
```

time: 506 us -> 275 us (0.54)
  the two profiles are of different devices: /device:TPU:1 before, /device:TPU:2 now
where the time goes in v1:
time: 275 us; the launch traced here: 274 us
  waiting for transfers between devices  154 us (56%)
  blocking collectives  43.2 us (16%)
  starting transfers between devices  39.8 us (14%)
  between operations  14.4 us (5%)
  matrix products  9.29 us (3%)
  local copies, waits for them, and re-layouts  8.03 us (3%)
  other arithmetic  5.14 us (2%)
    all_gather x1, waiting for transfers between devices, local(): lax.all_gather(jnp.concatenate([head_cotangents, attention_out], axis=1),...  76.7 us
    all_to_all x1, waiting for transfers between devices, local(): received = lax.all_to_all(partial, 'dp', 0, 0, tiled=True)  54.4 us
    all_gather x1, blocking collectives, local(): first = lax.all_gather(update_main[:cut], 'dp', axis=0)  43.2 us
    all_to_all x1, starting transfers between devices, local(): received = lax.all_to_all(partial, 'dp', 0, 0, tiled=True)  12.3 us
    all_to_all x1, waiting for transfers between devices, local(): lax.all_to_all(jnp.broadcast_to(summed[None, slab:], (per_extra, slab, he...  10.4 us
    all_to_all x1, starting transfers between devices, local(): lax.all_to_all(jnp.broadcast_to(tail[None], (groups,) + tail.shape), 'dp'...  8.51 us
    all_to_all x1, starting transfers between devices, local(): lax.all_to_all(jnp.broadcast_to(summed[None, slab:], (per_extra, slab, he...  8.3 us
    all_to_all x1, waiting for transfers between devices, local(): summed = jnp.sum(lax.all_to_all(both, 'fsdp', 0, 0, tiled=True), axis=0)  6.61 us
  transfers between devices with their start and end apart: 6, of which 5 were waited for; matrix products, arithmetic and copies ran while one was open for 1% of the time, Pallas kernels for 0%

profile of v1, /device:TPU:2, one launch (start us, length us, event | category | flops | bytes accessed | tf_op | source)
XLA Modules:
  0.0 274.0 jit_solution(13861149614078126977)
XLA Ops:
  6.5 1.8 pad_maximum_fusion.3
  9.0 76.7 %all-gather.3.cloned.1.call-done = bf16[2048,2304]{1,0:T(8,128)(2,1)} async-done(((bf16[64,2304]{1,0:T(8,128)(2,1)}), bf16[2048,2304]{1,0:T(8,128)(2,1)}) %all-gather.3.cloned.1.call-update) | async-done | bytes 9437200 | tf_op jit(solution)/shard_map/all_gather | solution.py:64
  85.7 4.0 %fusion.7 = bf16[256,1024]{1,0:T(8,128)(2,1)S(1)} fusion(bf16[2048,2304]{1,0:T(8,128)(2,1)} %all-gather.3.cloned.1.call-done, bf16[2048,256]{1,0:T(8,128)(2,1)} %param.7, bf16[2048]{0:T(1024)(128)(2,1)S(1)} %fusion.42), kind=kOutput, calls=%fused_computation.7 | convolution fusion | flops 1074528256 | bytes 5771264 | tf_op jit(solution)/shard_map/dot_general | solution.py:71
  89.7 1.2 copy-done
  91.0 1.7 fusion.4
  92.7 0.6 copy.37
  93.6 0.3 copy.39
  94.1 1.6 copy.40
  95.7 12.3 %all-to-all-start = ((bf16[16,288,128]{2,1,0:T(8,128)(2,1)}), bf16[16,288,128]{2,1,0:T(8,128)(2,1)S(1)}, u32[]{:S(2)}, u32[]{:S(2)}) async-start(bf16[16,288,128]{2,1,0:T(8,128)(2,1)} %copy.40), calls=%async_computation | async-start | bytes 2359296 | tf_op jit(solution)/shard_map/all_to_all | solution.py:79
  108.1 0.9 constant_dynamic-slice_fusion.1
  109.1 54.4 %all-to-all-done = bf16[16,288,128]{2,1,0:T(8,128)(2,1)S(1)} async-done(((bf16[16,288,128]{2,1,0:T(8,128)(2,1)}), bf16[16,288,128]{2,1,0:T(8,128)(2,1)S(1)}, u32[]{:S(2)}, u32[]{:S(2)}) %all-to-all-start) | async-done | bytes 1179680 | tf_op jit(solution)/shard_map/all_to_all | solution.py:79
  164.2 0.7 pad_maximum_fusion.4
  164.9 5.8 %all-to-all-start.1 = ((f32[32,8,128]{2,1,0:T(8,128)}), f32[32,8,128]{2,1,0:T(8,128)S(1)}, u32[]{:S(2)}, u32[]{:S(2)}) async-start(f32[32,8,128]{2,1,0:T(8,128)} %pad_maximum_fusion.4), calls=%async_computation.1 | async-start | bytes 262144 | tf_op jit(solution)/shard_map/all_to_all | solution.py:94
  170.7 6.6 %all-to-all-done.1 = f32[32,8,128]{2,1,0:T(8,128)S(1)} async-done(((f32[32,8,128]{2,1,0:T(8,128)}), f32[32,8,128]{2,1,0:T(8,128)S(1)}, u32[]{:S(2)}, u32[]{:S(2)}) %all-to-all-start.1) | async-done | bytes 131104 | tf_op jit(solution)/shard_map/all_to_all | solution.py:94
  177.4 0.6 broadcast_in_dim.6
  178.0 8.3 %all-to-all-start.2 = ((f32[8,4,128]{2,1,0:T(4,128)}), f32[8,4,128]{2,1,0:T(4,128)S(1)}, u32[]{:S(2)}, u32[]{:S(2)}) async-start(f32[8,4,128]{2,1,0:T(4,128)} %broadcast_in_dim.6), calls=%async_computation.2 | async-start | bytes 32768 | tf_op jit(solution)/shard_map/all_to_all | solution.py:97
  186.4 10.4 %all-to-all-done.2 = f32[8,4,128]{2,1,0:T(4,128)S(1)} async-done(((f32[8,4,128]{2,1,0:T(4,128)}), f32[8,4,128]{2,1,0:T(4,128)S(1)}, u32[]{:S(2)}, u32[]{:S(2)}) %all-to-all-start.2) | async-done | bytes 16416 | tf_op jit(solution)/shard_map/all_to_all | solution.py:97
  196.8 0.7 broadcast_in_dim.7
  197.5 4.9 %all-to-all-start.3 = ((f32[32,8,128]{2,1,0:T(8,128)}), f32[32,8,128]{2,1,0:T(8,128)S(1)}, u32[]{:S(2)}, u32[]{:S(2)}) async-start(f32[32,8,128]{2,1,0:T(8,128)} %broadcast_in_dim.7), calls=%async_computation.3 | async-start | bytes 262144 | tf_op jit(solution)/shard_map/all_to_all | solution.py:104
  202.4 0.6 slice.70
  203.0 6.1 %all-to-all-done.3 = f32[32,8,128]{2,1,0:T(8,128)S(1)} async-done(((f32[32,8,128]{2,1,0:T(8,128)}), f32[32,8,128]{2,1,0:T(8,128)S(1)}, u32[]{:S(2)}, u32[]{:S(2)}) %all-to-all-start.3) | async-done | bytes 131104 | tf_op jit(solution)/shard_map/all_to_all | solution.py:104
  209.4 0.4 fusion.12
  209.8 0.3 fusion.24
  210.4 0.3 fusion.11
  210.7 0.3 fusion.48
  210.9 0.7 multiply_bitcast_fusion
  211.6 0.3 fusion.22
  212.2 0.3 fusion.10
  213.5 0.8 broadcast_in_dim.8
  214.3 8.5 %all-to-all-start.4 = ((bf16[16,64,128]{2,1,0:T(8,128)(2,1)}), bf16[16,64,128]{2,1,0:T(8,128)(2,1)S(1)}, u32[]{:S(2)}, u32[]{:S(2)}) async-start(bf16[16,64,128]{2,1,0:T(8,128)(2,1)} %broadcast_in_dim.8), calls=%async_computation.4 | async-start | bytes 524288 | tf_op jit(solution)/shard_map/all_to_all | solution.py:116
  222.8 43.2 %all-gather = bf16[3584,128]{1,0:T(8,128)(2,1)S(1)} all-gather(bf16[224,128]{1,0:T(8,128)(2,1)S(1)} %slice.72), channel_id=2, replica_groups=mesh['dp'=16,'fsdp'=32] {'dp'}, dimensions={0}, use_global_device_ids=true | all-gather | bytes 974848 | tf_op jit(solution)/shard_map/all_gather | solution.py:114
  266.0 1.1 pad_maximum_fusion.2
  (49 shorter events, 3.4 us)
Async XLA Ops:
  6.5 79.2 %all-gather.3.cloned.1.call-start = ((), (), s32[]{:S(2)}) async-start(), calls=%async_computation.5 | async-start | bytes 9732096 | tf_op jit(solution)/shard_map/all_gather | solution.py:64
  6.5 83.2 %copy-start.1 = (bf16[2048,256]{1,0:T(8,128)(2,1)S(1)}, bf16[2048,256]{1,0:T(8,128)(2,1)}, u32[]{:S(2)}) copy-start(bf16[2048,256]{1,0:T(8,128)(2,1)} %param.6) | copy-start | bytes 3145732
  85.7 5.3 %copy-start = (bf16[2048,2304]{1,0:T(8,128)(2,1)S(1)}, bf16[2048,2304]{1,0:T(8,128)(2,1)}, u32[]{:S(2)}) copy-start(bf16[2048,2304]{1,0:T(8,128)(2,1)} %all-gather.3.cloned.1.call-done) | copy-start | bytes 28311556
  94.1 13.9 %slice-start = ((f32[18,256,128]{2,1,0:T(8,128)}), f32[2,256,128]{2,1,0:T(8,128)S(1)}, s32[]{:S(2)}) async-start(f32[18,256,128]{2,1,0:T(8,128)} %param.10), calls=%async_computation.6 | async-start | bytes 524288 | tf_op jit(solution)/shard_map/slice | solution.py:83
  95.7 67.8 %all-to-all-start = ((bf16[16,288,128]{2,1,0:T(8,128)(2,1)}), bf16[16,288,128]{2,1,0:T(8,128)(2,1)S(1)}, u32[]{:S(2)}, u32[]{:S(2)}) async-start(bf16[16,288,128]{2,1,0:T(8,128)(2,1)} %copy.40), calls=%async_computation | async-start | bytes 2359296 | tf_op jit(solution)/shard_map/all_to_all | solution.py:79
  164.9 12.4 %all-to-all-start.1 = ((f32[32,8,128]{2,1,0:T(8,128)}), f32[32,8,128]{2,1,0:T(8,128)S(1)}, u32[]{:S(2)}, u32[]{:S(2)}) async-start(f32[32,8,128]{2,1,0:T(8,128)} %pad_maximum_fusion.4), calls=%async_computation.1 | async-start | bytes 262144 | tf_op jit(solution)/shard_map/all_to_all | solution.py:94
  178.0 18.8 %all-to-all-start.2 = ((f32[8,4,128]{2,1,0:T(4,128)}), f32[8,4,128]{2,1,0:T(4,128)S(1)}, u32[]{:S(2)}, u32[]{:S(2)}) async-start(f32[8,4,128]{2,1,0:T(4,128)} %broadcast_in_dim.6), calls=%async_computation.2 | async-start | bytes 32768 | tf_op jit(solution)/shard_map/all_to_all | solution.py:97
  197.5 11.7 %all-to-all-start.3 = ((f32[32,8,128]{2,1,0:T(8,128)}), f32[32,8,128]{2,1,0:T(8,128)S(1)}, u32[]{:S(2)}, u32[]{:S(2)}) async-start(f32[32,8,128]{2,1,0:T(8,128)} %broadcast_in_dim.7), calls=%async_computation.3 | async-start | bytes 262144 | tf_op jit(solution)/shard_map/all_to_all | solution.py:104
  214.3 51.7 %all-to-all-start.4 = ((bf16[16,64,128]{2,1,0:T(8,128)(2,1)}), bf16[16,64,128]{2,1,0:T(8,128)(2,1)S(1)}, u32[]{:S(2)}, u32[]{:S(2)}) async-start(bf16[16,64,128]{2,1,0:T(8,128)(2,1)} %broadcast_in_dim.8), calls=%async_computation.4 | async-start | bytes 524288 | tf_op jit(solution)/shard_map/all_to_all | solution.py:116
Sparse Core Ops, SparseCore 0:
  10.5 75.1 all-gather.2

commit v2 on v1

v2 whole, which is shorter than its diff:
```python
import math

import jax
import jax.numpy as jnp
from jax import lax
from jax.sharding import PartitionSpec as P

ITERS = 3
EARLY = 32


coef_a = 3.4445
coef_b = -4.775
coef_c = 2.0315
momentum_decay = 0.95
update_gain = 0.2
norm_floor = 1e-07


def nesterov_blend(gradient, moment_rows):
    new_moment = momentum_decay * moment_rows + gradient
    return (gradient + momentum_decay * new_moment).astype(jnp.bfloat16)


def poly_of_gram(gram, out_scale):
    highest = lax.Precision.HIGHEST

    def mul(left, right):
        return jnp.einsum("mij,mjk->mik", left, right, precision=highest)

    size = gram.shape[-1]
    eye = jnp.eye(size, dtype=jnp.float32)[None]
    sum_squares = jnp.sum(gram * eye, axis=(1, 2), keepdims=True)
    inverse = 1.0 / (jnp.sqrt(sum_squares) + norm_floor)
    current = gram * inverse * inverse
    factor = eye * (inverse * out_scale)
    for iteration in range(ITERS):
        step = coef_a * eye + coef_b * current + coef_c * mul(current, current)
        factor = mul(factor, step) if iteration else factor[:, :1, :1] * step
        if iteration < ITERS - 1:
            current = mul(mul(current, step), step)
    return factor


def split_product(columns, factor):
    high = lax.reduce_precision(factor, 8, 7)
    contract = (((0,), (0,)), ((), ()))
    parts = [
        lax.dot_general(columns, part.astype(jnp.bfloat16), contract, preferred_element_type=jnp.float32)
        for part in (high, factor - high)
    ]
    return (parts[0] + parts[1]).astype(jnp.bfloat16)


def local(features, out_cotangent, head_cotangents, attention_out, momentum, lengths):
    tok_count, row_count = features.shape
    mat_count, _, head_size = momentum.shape
    groups, owners = lax.axis_size("dp"), lax.axis_size("fsdp")
    own_tok = head_cotangents.shape[0]
    in_mats = head_cotangents.shape[1] // head_size
    out_mats = groups - in_mats
    extra = mat_count - groups
    share = extra * head_size // groups
    cores = 2
    places = owners // cores
    group, core = lax.axis_index("dp"), lax.axis_index("fsdp") % cores
    same_core = [list(range(c, owners, cores)) for c in range(cores)]
    across = [(i, i ^ 1) for i in range(owners)]

    head3 = head_cotangents.reshape(own_tok, in_mats, head_size)
    attn3 = attention_out.reshape(own_tok, mat_count - in_mats, head_size)

    def pick(low, high):
        return [
            head3[:, :, low:high].reshape(own_tok, in_mats * (high - low)),
            attn3[:, :out_mats, low:high].reshape(own_tok, out_mats * (high - low)),
        ]

    late_heads = lax.all_gather(
        jnp.concatenate(pick(EARLY, head_size), axis=1), "fsdp", axis=0, tiled=True
    )
    early_own = jnp.concatenate(
        pick(0, EARLY) + [attn3[:, out_mats:].reshape(own_tok, extra * head_size)], axis=1
    )
    mine = lax.all_to_all(
        jnp.broadcast_to(early_own[None], (places,) + early_own.shape),
        "fsdp", 0, 0, axis_index_groups=same_core, tiled=True,
    ).reshape(places * own_tok, early_own.shape[1])
    other = lax.ppermute(mine, "fsdp", across)

    live_mask = (lax.iota(jnp.int32, tok_count) < lengths[0]).astype(jnp.bfloat16)[:, None]

    def halves(rows):
        split = (rows * live_mask).reshape(places, cores, own_tok, row_count)
        return [
            lax.dynamic_index_in_dim(split, which, 1, keepdims=False).reshape(-1, row_count)
            for which in (core, 1 - core)
        ]

    def product(heads, rows):
        contract = (((0,), (0,)), ((), ()))
        return lax.dot_general(heads, rows, contract, preferred_element_type=jnp.float32)

    feature_halves, cotangent_halves = halves(features), halves(out_cotangent)
    cut = in_mats * EARLY
    early_in = product(mine[:, :cut], feature_halves[0]) + product(other[:, :cut], feature_halves[1])
    early_out = product(mine[:, cut:], cotangent_halves[0]) + product(other[:, cut:], cotangent_halves[1])
    early = jnp.concatenate([early_in, early_out], axis=0).astype(jnp.bfloat16)
    early = jnp.concatenate(
        [
            early[: groups * EARLY].reshape(groups, EARLY, row_count),
            early[groups * EARLY :].reshape(groups, share, row_count),
        ],
        axis=1,
    )
    early = lax.all_to_all(early, "dp", 0, 0, tiled=True)

    cut = in_mats * (head_size - EARLY)
    late_in = product(late_heads[:, :cut], features * live_mask)
    late_out = product(late_heads[:, cut:], out_cotangent * live_mask)
    late = jnp.concatenate([late_in, late_out], axis=0).astype(jnp.bfloat16)
    early, late = lax.optimization_barrier((early, late))
    early_sum = jnp.sum(early.astype(jnp.float32), axis=0)

    moment_main = lax.dynamic_index_in_dim(momentum, group, 0, keepdims=False).T
    moment_rest = lax.dynamic_index_in_dim(
        momentum[groups:].transpose(0, 2, 1).reshape(groups, share, row_count), group, 0, keepdims=False
    )
    rest = nesterov_blend(early_sum[EARLY:], moment_rest)

    late = late.reshape(groups, head_size - EARLY, row_count)
    late = jnp.concatenate([late, jnp.broadcast_to(rest[None], (groups, share, row_count))], axis=1)
    late = lax.all_to_all(late, "dp", 0, 0, tiled=True)
    late_sum = jnp.sum(late[:, : head_size - EARLY].astype(jnp.float32), axis=0)
    rest = late[:, head_size - EARLY :].reshape(extra, head_size, row_count)
    main = jnp.concatenate(
        [
            nesterov_blend(early_sum[:EARLY], moment_main[:EARLY]),
            nesterov_blend(late_sum, moment_main[EARLY:]),
        ],
        axis=0,
    )

    def gram(columns):
        return lax.dot_general(columns, columns, (((1,), (1,)), ((), ())), preferred_element_type=jnp.float32)

    slab = head_size // owners
    blended = [main] + [rest[e] for e in range(extra)]
    grams = jnp.stack([gram(b).reshape(owners, slab, head_size) for b in blended], axis=1)
    grams = grams.reshape(owners, (1 + extra) * slab, head_size)
    summed = jnp.sum(lax.all_to_all(grams, "fsdp", 0, 0, tiled=True), axis=0)
    grams = lax.all_to_all(jnp.broadcast_to(summed[None], grams.shape), "fsdp", 0, 0, tiled=True)
    grams = grams.reshape(owners, 1 + extra, slab, head_size).transpose(1, 0, 2, 3)
    out_scale = update_gain * math.sqrt(max(row_count * owners, head_size))
    factors = poly_of_gram(grams.reshape(1 + extra, head_size, head_size), out_scale)
    update = split_product(main, factors[0])
    cut = row_count - row_count // groups
    tail = jnp.broadcast_to(update[None, cut:], (groups, row_count - cut, head_size))
    tails = lax.all_to_all(tail, "dp", 0, 0, tiled=True)
    updates = lax.all_gather(update[:cut], "dp", axis=0)
    rests = jnp.stack([split_product(rest[e], factors[1 + e]) for e in range(extra)])
    return jnp.concatenate([jnp.concatenate([updates, tails], axis=1), rests], axis=0)


def solution(mesh):
    return jax.shard_map(
        local,
        mesh=mesh,
        in_specs=(
            P("dp", "fsdp"),
            P("dp", "fsdp"),
            P(("dp", "fsdp"), None),
            P(("dp", "fsdp"), None),
            P(None, "fsdp", None),
            P("dp"),
        ),
        out_specs=P(None, "fsdp", None),
        check_vma=False,
    )
```

time: 275 us -> 233 us (0.85)
  waiting for transfers between devices: 154 us -> 79.3 us
  blocking collectives: 43.2 us -> 66.8 us
  matrix products: 9.29 us -> 17 us
    all_gather x1, waiting for transfers between devices: 76.7 us -> 11.6 us  [local(): lax.all_gather(jnp.concatenate(pick(EARLY, head_size), axis=1), 'fsdp', a...]
    all_to_all x0 -> x1, blocking collectives: none -> 30.2 us  [local(): lax.all_to_all(jnp.broadcast_to(early_own[None], (places,) + early_own.sh...]
    all_to_all x5, waiting for transfers between devices: 77.5 us -> 67.7 us  [the longest x1 43.7 us: local(): late = lax.all_to_all(late, 'dp', 0, 0, tiled=True)]
    dot_general x8 -> x15, matrix products: 6.69 us -> 13.8 us  [the longest x6 12.2 us: product(): lax.dot_general(heads, rows, contract, preferred_element_type=jnp.float32)]
    all_gather x1, blocking collectives: 43.2 us -> 36.6 us  [local(): updates = lax.all_gather(update[:cut], 'dp', axis=0)]
  transfers between devices with their start and end apart: 6 -> 7, of which waited for: 5 -> 5; matrix products, arithmetic and copies ran while one was open for 1% -> 7% of each run, Pallas kernels for 0% -> 0%
where the time goes in v2:
time: 233 us; the launch traced here: 232 us
  waiting for transfers between devices  79.3 us (34%)
  blocking collectives  66.8 us (29%)
  starting transfers between devices  41.3 us (18%)
  matrix products  17 us (7%)
  between operations  14.5 us (6%)
  local copies, waits for them, and re-layouts  6.92 us (3%)
  other arithmetic  6.52 us (3%)
    all_to_all x1, waiting for transfers between devices, local(): late = lax.all_to_all(late, 'dp', 0, 0, tiled=True)  43.7 us
    all_gather x1, blocking collectives, local(): updates = lax.all_gather(update[:cut], 'dp', axis=0)  36.6 us
    all_to_all x1, blocking collectives, local(): lax.all_to_all(jnp.broadcast_to(early_own[None], (places,) + early_own.sh...  30.2 us
    all_to_all x1, starting transfers between devices, local(): early = lax.all_to_all(early, 'dp', 0, 0, tiled=True)  16.1 us
    dot_general x6, matrix products, product(): lax.dot_general(heads, rows, contract, preferred_element_type=jnp.float32)  12.2 us
    all_gather x1, waiting for transfers between devices, local(): lax.all_gather(jnp.concatenate(pick(EARLY, head_size), axis=1), 'fsdp', a...  11.6 us
    all_to_all x1, waiting for transfers between devices, local(): early = lax.all_to_all(early, 'dp', 0, 0, tiled=True)  8.62 us
    all_to_all x1, starting transfers between devices, local(): tails = lax.all_to_all(tail, 'dp', 0, 0, tiled=True)  7.78 us
  transfers between devices with their start and end apart: 7, of which 5 were waited for; matrix products, arithmetic and copies ran while one was open for 7% of the time, Pallas kernels for 0%

profile of v2, /device:TPU:2, one launch (start us, length us, event | category | flops | bytes accessed | tf_op | source)
XLA Modules:
  0.0 232.3 jit_solution(1111824476368001862)
XLA Ops:
  6.5 0.9 copy.32
  7.5 1.0 reshape.131
  9.1 0.8 pad_maximum_fusion.6
  10.7 30.2 %all_to_all.30 = bf16[16,64,768]{2,1,0:T(8,128)(2,1)} all-to-all(bf16[16,64,768]{2,1,0:T(8,128)(2,1)S(1)} %broadcast_in_dim.8), channel_id=1, replica_groups={{0,2,4,6,8,10,12,14,16,18,20,22,24,26,28,30},{1,3,5,7,9,11,13,15,17,19,..., dimensions={0} | all-to-all | bytes 3145728 | tf_op jit(solution)/shard_map/all_to_all | solution.py:85
  40.9 1.9 collective-permute-start
  43.5 1.6 broadcast_multiply_fusion.1
  45.4 1.5 fusion.24
  46.9 2.1 fusion.21
  49.0 2.1 fusion.10
  51.1 1.6 fusion.11
  52.7 0.8 pad_maximum_fusion.3
  53.5 16.1 %all-to-all-start.1 = ((bf16[16,48,256]{2,1,0:T(8,128)(2,1)}), bf16[16,48,256]{2,1,0:T(8,128)(2,1)S(1)}, u32[]{:S(2)}, u32[]{:S(2)}) async-start(bf16[16,48,256]{2,1,0:T(8,128)(2,1)} %pad_maximum_fusion.3), calls=%async_computation.1 | async-start | bytes 786432 | tf_op jit(solution)/shard_map/all_to_all | solution.py:116
  69.7 11.6 %all-gather.3.cloned.1.call-done = bf16[2048,1536]{1,0:T(8,128)(2,1)} async-done(((bf16[64,1536]{1,0:T(8,128)(2,1)}), bf16[2048,1536]{1,0:T(8,128)(2,1)}) %all-gather.3.cloned.1.call-update) | async-done | bytes 6291472 | tf_op jit(solution)/shard_map/all_gather | solution.py:79
  81.3 3.6 %fusion.7 = bf16[576,256]{1,0:T(8,128)(2,1)S(1)} fusion(bf16[2048,256]{1,0:T(8,128)(2,1)S(1)} %get-tuple-element.18, bf16[2048,1536]{1,0:T(8,128)(2,1)} %all-gather.3.cloned.1.call-done), kind=kOutput, calls=%fused_computation.7 | convolution fusion | flops 604127232 | bytes 3964928 | tf_op jit(solution)/shard_map/dot_general | solution.py:102
  84.9 1.4 fusion.4
  86.3 8.6 %all-to-all-done.1 = bf16[16,48,256]{2,1,0:T(8,128)(2,1)S(1)} async-done(((bf16[16,48,256]{2,1,0:T(8,128)(2,1)}), bf16[16,48,256]{2,1,0:T(8,128)(2,1)S(1)}, u32[]{:S(2)}, u32[]{:S(2)}) %all-to-all-start.1) | async-done | bytes 393248 | tf_op jit(solution)/shard_map/all_to_all | solution.py:116
  95.1 1.0 pad_maximum_fusion.1
  96.1 5.2 %all-to-all-start.2 = ((bf16[16,112,256]{2,1,0:T(8,128)(2,1)}), bf16[16,112,256]{2,1,0:T(8,128)(2,1)S(1)}, u32[]{:S(2)}, u32[]{:S(2)}) async-start(bf16[16,112,256]{2,1,0:T(8,128)(2,1)} %pad_maximum_fusion.1), calls=%async_computation.2 | async-start | bytes 1835008 | tf_op jit(solution)/shard_map/all_to_all | solution.py:133
  101.4 0.6 slice.135
  102.0 43.7 %all-to-all-done.2 = bf16[16,112,256]{2,1,0:T(8,128)(2,1)S(1)} async-done(((bf16[16,112,256]{2,1,0:T(8,128)(2,1)}), bf16[16,112,256]{2,1,0:T(8,128)(2,1)S(1)}, u32[]{:S(2)}, u32[]{:S(2)}) %all-to-all-start.2) | async-done | bytes 917536 | tf_op jit(solution)/shard_map/all_to_all | solution.py:133
  146.4 0.8 copy.28
  147.3 5.4 %all-to-all-start.3 = ((f32[32,12,128]{2,1,0:T(8,128)}), f32[32,12,128]{2,1,0:T(8,128)S(1)}, u32[]{:S(2)}, u32[]{:S(2)}) async-start(f32[32,12,128]{2,1,0:T(8,128)} %copy.28), calls=%async_computation.3 | async-start | bytes 524288 | tf_op jit(solution)/shard_map/all_to_all | solution.py:151
  152.7 7.7 %all-to-all-done.3 = f32[32,12,128]{2,1,0:T(8,128)S(1)} async-done(((f32[32,12,128]{2,1,0:T(8,128)}), f32[32,12,128]{2,1,0:T(8,128)S(1)}, u32[]{:S(2)}, u32[]{:S(2)}) %all-to-all-start.3) | async-done | bytes 196640 | tf_op jit(solution)/shard_map/all_to_all | solution.py:151
  160.4 0.7 broadcast_in_dim.10
  161.1 5.0 %all-to-all-start.4 = ((f32[32,12,128]{2,1,0:T(8,128)}), f32[32,12,128]{2,1,0:T(8,128)S(1)}, u32[]{:S(2)}, u32[]{:S(2)}) async-start(f32[32,12,128]{2,1,0:T(8,128)} %broadcast_in_dim.10), calls=%async_computation.4 | async-start | bytes 524288 | tf_op jit(solution)/shard_map/all_to_all | solution.py:152
  166.2 7.7 %all-to-all-done.4 = f32[32,12,128]{2,1,0:T(8,128)S(1)} async-done(((f32[32,12,128]{2,1,0:T(8,128)}), f32[32,12,128]{2,1,0:T(8,128)S(1)}, u32[]{:S(2)}, u32[]{:S(2)}) %all-to-all-start.4) | async-done | bytes 196640 | tf_op jit(solution)/shard_map/all_to_all | solution.py:152
  174.3 0.4 fusion.14
  176.1 0.6 multiply_bitcast_fusion
  178.8 0.7 broadcast_in_dim.11
  179.4 7.8 %all-to-all-start.5 = ((bf16[16,16,128]{2,1,0:T(8,128)(2,1)}), bf16[16,16,128]{2,1,0:T(8,128)(2,1)S(1)}, u32[]{:S(2)}, u32[]{:S(2)}) async-start(bf16[16,16,128]{2,1,0:T(8,128)(2,1)} %broadcast_in_dim.11), calls=%async_computation.5 | async-start | bytes 131072 | tf_op jit(solution)/shard_map/all_to_all | solution.py:159
  187.2 36.6 %all-gather = bf16[3840,128]{1,0:T(8,128)(2,1)S(1)} all-gather(bf16[240,128]{1,0:T(8,128)(2,1)S(1)} %slice.137), channel_id=2, replica_groups=mesh['dp'=16,'fsdp'=32] {'dp'}, dimensions={0}, use_global_device_ids=true | all-gather | bytes 1044480 | tf_op jit(solution)/shard_map/all_gather | solution.py:160
  224.4 1.1 pad_maximum_fusion
  (70 shorter events, 7.2 us)
Async XLA Ops:
  6.5 74.8 %all-gather.3.cloned.1.call-start = ((), (), s32[]{:S(2)}) async-start(), calls=%async_computation.6 | async-start | bytes 6488064 | tf_op jit(solution)/shard_map/all_gather | solution.py:79
  10.7 32.8 %copy-start = (bf16[2048,256]{1,0:T(8,128)(2,1)S(1)}, bf16[2048,256]{1,0:T(8,128)(2,1)}, u32[]{:S(2)}) copy-start(bf16[2048,256]{1,0:T(8,128)(2,1)} %param.6) | copy-start | bytes 3145732
  40.9 8.1 %collective-permute-start = (bf16[1024,768]{1,0:T(8,128)(2,1)}, bf16[1024,768]{1,0:T(8,128)(2,1)}, u32[]{:S(2)}, u32[]{:S(2)}) collective-permute-start(bf16[1024,768]{1,0:T(8,128)(2,1)} %bitcast.3), channel_id=1, source_target_pairs={{0,1},{1,0},{2,3},{3,2},{4,5},{5,4},{6,7},{7,6},{8,9},{9,8},{10,11... | collective-permute-start | bytes 4718600 | tf_op jit(solution)/shard_map/ppermute | solution.py:89
  52.7 16.9 %slice-start = ((f32[18,256,128]{2,1,0:T(8,128)}), f32[2,256,128]{2,1,0:T(8,128)S(1)}, s32[]{:S(2)}) async-start(f32[18,256,128]{2,1,0:T(8,128)} %param.10), calls=%async_computation.7 | async-start | bytes 524288 | tf_op jit(solution)/shard_map/slice | solution.py:127
  53.5 41.5 %all-to-all-start.1 = ((bf16[16,48,256]{2,1,0:T(8,128)(2,1)}), bf16[16,48,256]{2,1,0:T(8,128)(2,1)S(1)}, u32[]{:S(2)}, u32[]{:S(2)}) async-start(bf16[16,48,256]{2,1,0:T(8,128)(2,1)} %pad_maximum_fusion.3), calls=%async_computation.1 | async-start | bytes 786432 | tf_op jit(solution)/shard_map/all_to_all | solution.py:116
  81.3 3.6 %copy-start.2 = (bf16[2048,1536]{1,0:T(8,128)(2,1)S(1)}, bf16[2048,1536]{1,0:T(8,128)(2,1)}, u32[]{:S(2)}) copy-start(bf16[2048,1536]{1,0:T(8,128)(2,1)} %all-gather.3.cloned.1.call-done) | copy-start | bytes 18874372
  95.1 6.2 %copy-start.1 = (f32[18,256,128]{2,1,0:T(8,128)S(1)}, f32[18,256,128]{2,1,0:T(8,128)}, u32[]{:S(2)}) copy-start(f32[18,256,128]{2,1,0:T(8,128)} %param.10) | copy-start | bytes 7077892
  96.1 49.6 %all-to-all-start.2 = ((bf16[16,112,256]{2,1,0:T(8,128)(2,1)}), bf16[16,112,256]{2,1,0:T(8,128)(2,1)S(1)}, u32[]{:S(2)}, u32[]{:S(2)}) async-start(bf16[16,112,256]{2,1,0:T(8,128)(2,1)} %pad_maximum_fusion.1), calls=%async_computation.2 | async-start | bytes 1835008 | tf_op jit(solution)/shard_map/all_to_all | solution.py:133
  147.3 13.1 %all-to-all-start.3 = ((f32[32,12,128]{2,1,0:T(8,128)}), f32[32,12,128]{2,1,0:T(8,128)S(1)}, u32[]{:S(2)}, u32[]{:S(2)}) async-start(f32[32,12,128]{2,1,0:T(8,128)} %copy.28), calls=%async_computation.3 | async-start | bytes 524288 | tf_op jit(solution)/shard_map/all_to_all | solution.py:151
  161.1 12.8 %all-to-all-start.4 = ((f32[32,12,128]{2,1,0:T(8,128)}), f32[32,12,128]{2,1,0:T(8,128)S(1)}, u32[]{:S(2)}, u32[]{:S(2)}) async-start(f32[32,12,128]{2,1,0:T(8,128)} %broadcast_in_dim.10), calls=%async_computation.4 | async-start | bytes 524288 | tf_op jit(solution)/shard_map/all_to_all | solution.py:152
  179.4 45.0 %all-to-all-start.5 = ((bf16[16,16,128]{2,1,0:T(8,128)(2,1)}), bf16[16,16,128]{2,1,0:T(8,128)(2,1)S(1)}, u32[]{:S(2)}, u32[]{:S(2)}) async-start(bf16[16,16,128]{2,1,0:T(8,128)(2,1)} %broadcast_in_dim.11), calls=%async_computation.5 | async-start | bytes 131072 | tf_op jit(solution)/shard_map/all_to_all | solution.py:159
Sparse Core Ops, SparseCore 0:
  10.5 70.7 all-gather.2

commit v3 on v2

v3 whole, which is shorter than its diff:
```python
import math

import jax
import jax.numpy as jnp
from jax import lax
from jax.sharding import Mesh
from jax.sharding import PartitionSpec as P

ITERS = 3
EARLY = 32


coef_a = 3.4445
coef_b = -4.775
coef_c = 2.0315
momentum_decay = 0.95
update_gain = 0.2
norm_floor = 1e-07


def nesterov_blend(gradient, moment_rows):
    new_moment = momentum_decay * moment_rows + gradient
    return (gradient + momentum_decay * new_moment).astype(jnp.bfloat16)


def poly_of_gram(gram, out_scale):
    highest = lax.Precision.HIGHEST

    def mul(left, right):
        return jnp.einsum("mij,mjk->mik", left, right, precision=highest)

    size = gram.shape[-1]
    eye = jnp.eye(size, dtype=jnp.float32)[None]
    sum_squares = jnp.sum(gram * eye, axis=(1, 2), keepdims=True)
    inverse = 1.0 / (jnp.sqrt(sum_squares) + norm_floor)
    current = gram * inverse * inverse
    factor = eye * (inverse * out_scale)
    for iteration in range(ITERS):
        step = coef_a * eye + coef_b * current + coef_c * mul(current, current)
        factor = mul(factor, step) if iteration else factor[:, :1, :1] * step
        if iteration < ITERS - 1:
            current = mul(mul(current, step), step)
    return factor


def split_product(columns, factor):
    high = lax.reduce_precision(factor, 8, 7)
    contract = (((0,), (0,)), ((), ()))
    parts = [
        lax.dot_general(columns, part.astype(jnp.bfloat16), contract, preferred_element_type=jnp.float32)
        for part in (high, factor - high)
    ]
    return (parts[0] + parts[1]).astype(jnp.bfloat16)


def local(features, out_cotangent, head_cotangents, attention_out, momentum, lengths):
    tok_count, row_count = features.shape
    mat_count, _, head_size = momentum.shape
    own_tok = head_cotangents.shape[0]
    pairs, places = lax.axis_size("pair"), lax.axis_size("place")
    cores = lax.axis_size("core")
    groups, owners = 2 * pairs, places * cores
    in_mats = head_cotangents.shape[1] // head_size
    share = head_size // pairs
    late_width = head_size - EARLY
    pair, side, core = lax.axis_index("pair"), lax.axis_index("side"), lax.axis_index("core")

    def exchange(array, axis):
        return lax.ppermute(array, axis, [(0, 1), (1, 0)])

    def product(heads, rows):
        contract = (((0,), (0,)), ((), ()))
        return lax.dot_general(heads, rows, contract, preferred_element_type=jnp.float32)

    heads = jnp.concatenate([head_cotangents, attention_out], axis=1).reshape(own_tok, mat_count, head_size)
    late_heads = lax.all_gather(
        heads[:, :groups, EARLY:].reshape(own_tok, groups * late_width), ("place", "core"), axis=0, tiled=True
    )

    early_own = jnp.concatenate(
        [
            heads[:, :groups, :EARLY].reshape(own_tok, groups * EARLY),
            heads[:, groups:].reshape(own_tok, (mat_count - groups) * head_size),
        ],
        axis=1,
    )
    mine = lax.all_to_all(
        jnp.broadcast_to(early_own[None], (places,) + early_own.shape), "place", 0, 0, tiled=True
    ).reshape(places * own_tok, early_own.shape[1])
    live_mask = (lax.iota(jnp.int32, tok_count) < lengths[0]).astype(jnp.bfloat16)[:, None]
    rows_in, rows_out = features * live_mask, out_cotangent * live_mask

    def halves(rows):
        split = rows.reshape(places, cores, own_tok, row_count)
        return [
            lax.dynamic_index_in_dim(split, which, 1, keepdims=False).reshape(-1, row_count)
            for which in (core, 1 - core)
        ]

    halves_in, halves_out = halves(rows_in), halves(rows_out)
    mine, halves_in, halves_out = lax.optimization_barrier((mine, halves_in, halves_out))
    other = exchange(mine, "core")
    cut = in_mats * EARLY
    early_in = product(mine[:, :cut], halves_in[0]) + product(other[:, :cut], halves_in[1])
    early_out = product(mine[:, cut:], halves_out[0]) + product(other[:, cut:], halves_out[1])
    early = jnp.concatenate([early_in, early_out], axis=0).astype(jnp.bfloat16)
    rest = early[groups * EARLY :].reshape(2, pairs, share, row_count).transpose(1, 0, 2, 3)
    early = jnp.concatenate(
        [early[: groups * EARLY].reshape(groups, EARLY, row_count), rest.reshape(groups, share, row_count)], axis=1
    )
    early = lax.all_to_all(early, ("pair", "side"), 0, 0, tiled=True)

    cut = in_mats * late_width
    late = jnp.concatenate(
        [
            product(late_heads[:, :cut], features * live_mask),
            product(late_heads[:, cut:], out_cotangent * live_mask),
        ],
        axis=0,
    ).reshape(pairs, 2, late_width, row_count)
    keep = jnp.where(side == 0, late[:, 0], late[:, 1])
    give = jnp.where(side == 0, late[:, 1], late[:, 0]).astype(jnp.bfloat16)
    early, keep, give = lax.optimization_barrier((early, keep, give))
    got = exchange(give, "side")
    late = (keep + got.astype(jnp.float32)).astype(jnp.bfloat16)
    early_sum = jnp.sum(early.astype(jnp.float32), axis=0)

    moment_main = lax.dynamic_index_in_dim(momentum, 2 * pair + side, 0, keepdims=False).T
    moment_rest = lax.dynamic_index_in_dim(momentum, groups + side, 0, keepdims=False).T
    moment_rest = lax.dynamic_slice_in_dim(moment_rest, pair * share, share, axis=0)
    rest = nesterov_blend(early_sum[EARLY:], moment_rest)

    late = jnp.concatenate([late, jnp.broadcast_to(rest[None], (pairs, share, row_count))], axis=1)
    late = lax.all_to_all(late, "pair", 0, 0, tiled=True)
    late_sum = jnp.sum(late[:, :late_width].astype(jnp.float32), axis=0)
    rest = late[:, late_width:].reshape(head_size, row_count)
    main = jnp.concatenate(
        [
            nesterov_blend(early_sum[:EARLY], moment_main[:EARLY]),
            nesterov_blend(late_sum, moment_main[EARLY:]),
        ],
        axis=0,
    )

    def gram(columns):
        return lax.dot_general(columns, columns, (((1,), (1,)), ((), ())), preferred_element_type=jnp.float32)

    slab = head_size // owners
    grams = jnp.concatenate([gram(b).reshape(owners, slab, head_size) for b in (main, rest)], axis=1)
    summed = jnp.sum(lax.all_to_all(grams, ("place", "core"), 0, 0, tiled=True), axis=0)
    grams = lax.all_to_all(jnp.broadcast_to(summed[None], grams.shape), ("place", "core"), 0, 0, tiled=True)
    grams = grams.reshape(owners, 2, slab, head_size).transpose(1, 0, 2, 3)
    out_scale = update_gain * math.sqrt(max(row_count * owners, head_size))
    factors = poly_of_gram(grams.reshape(2, head_size, head_size), out_scale)
    update = split_product(main, factors[0])
    here = split_product(rest, factors[1])
    there = exchange(here, "side")
    cut = row_count - row_count // groups
    tail = jnp.broadcast_to(update[None, cut:], (groups, row_count - cut, head_size))
    tails = lax.all_to_all(tail, ("pair", "side"), 0, 0, tiled=True)
    updates = lax.all_gather(update[:cut], ("pair", "side"), axis=0)
    last = jnp.stack([jnp.where(side == 0, here, there), jnp.where(side == 0, there, here)])
    return jnp.concatenate([jnp.concatenate([updates, tails], axis=1), last], axis=0)


def solution(mesh):
    groups, owners = mesh.devices.shape
    split = Mesh(mesh.devices.reshape(groups // 2, 2, owners // 2, 2), ("pair", "side", "place", "core"))
    dp, fsdp = ("pair", "side"), ("place", "core")
    return jax.shard_map(
        local,
        mesh=split,
        in_specs=(P(dp, fsdp), P(dp, fsdp), P(dp + fsdp, None), P(dp + fsdp, None), P(None, fsdp, None), P(dp)),
        out_specs=P(None, fsdp, None),
        check_vma=False,
    )
```

time: 233 us -> 232 us (level)
  blocking collectives: 66.8 us -> 36.1 us
  starting transfers between devices: 41.3 us -> 59.8 us
  other arithmetic: 6.52 us -> 12.4 us
  waiting for transfers between devices: 79.3 us -> 83.1 us
    all_to_all x1 -> x0, blocking collectives: 30.2 us -> none  [local(): lax.all_to_all(jnp.broadcast_to(early_own[None], (places,) + early_own.sh...]
    all_to_all x5 -> x6, starting transfers between devices: 39.4 us -> 54.1 us  [the longest x1 14.6 us: local(): early = lax.all_to_all(early, ('pair', 'side'), 0, 0, tiled=True)]
    all_to_all x5 -> x6, waiting for transfers between devices: 67.7 us -> 58.4 us  [the longest x1 27.1 us: local(): late = lax.all_to_all(late, 'pair', 0, 0, tiled=True)]
    ppermute x1 -> x3, waiting for transfers between devices: 0.01 us -> 7.86 us  [exchange(): return lax.ppermute(array, axis, [(0, 1), (1, 0)])]
    all_gather x1, waiting for transfers between devices: 11.6 us -> 16.8 us  [local(): lax.all_gather(heads[:, :groups, EARLY:].reshape(own_tok, groups * late_w...]
    ppermute x1 -> x3, starting transfers between devices: 1.91 us -> 5.74 us  [exchange(): return lax.ppermute(array, axis, [(0, 1), (1, 0)])]
  transfers between devices with their start and end apart: 7 -> 10, of which waited for: 5 -> 7; matrix products, arithmetic and copies ran while one was open for 7% -> 10% of each run, Pallas kernels for 0% -> 0%
where the time goes in v3:
time: 232 us; the launch traced here: 231 us
  waiting for transfers between devices  83.1 us (36%)
  starting transfers between devices  59.8 us (26%)
  blocking collectives  36.1 us (16%)
  matrix products  16.3 us (7%)
  between operations  14.5 us (6%)
  other arithmetic  12.4 us (5%)
  local copies, waits for them, and re-layouts  8.62 us (4%)
    all_gather x1, blocking collectives, local(): updates = lax.all_gather(update[:cut], ('pair', 'side'), axis=0)  36.1 us
    all_to_all x1, waiting for transfers between devices, local(): late = lax.all_to_all(late, 'pair', 0, 0, tiled=True)  27.1 us
    all_gather x1, waiting for transfers between devices, local(): lax.all_gather(heads[:, :groups, EARLY:].reshape(own_tok, groups * late_w...  16.8 us
    all_to_all x1, waiting for transfers between devices, local(): lax.all_to_all(jnp.broadcast_to(early_own[None], (places,) + early_own.sh...  16.2 us
    all_to_all x1, starting transfers between devices, local(): early = lax.all_to_all(early, ('pair', 'side'), 0, 0, tiled=True)  14.6 us
    dot_general x6, matrix products, product(): lax.dot_general(heads, rows, contract, preferred_element_type=jnp.float32)  12.7 us
    all_to_all x1, starting transfers between devices, local(): late = lax.all_to_all(late, 'pair', 0, 0, tiled=True)  12.2 us
    all_to_all x1, starting transfers between devices, local(): lax.all_to_all(jnp.broadcast_to(early_own[None], (places,) + early_own.sh...  10 us
  transfers between devices with their start and end apart: 10, of which 7 were waited for; matrix products, arithmetic and copies ran while one was open for 10% of the time, Pallas kernels for 0%

profile of v3, /device:TPU:2, one launch (start us, length us, event | category | flops | bytes accessed | tf_op | source)
XLA Modules:
  0.0 230.9 jit_solution(6655332759931117349)
XLA Ops:
  6.5 1.1 pad_maximum_fusion.4
  9.6 1.4 broadcast_in_dim.8
  11.0 10.0 %all-to-all-start = ((bf16[16,64,768]{2,1,0:T(8,128)(2,1)}), bf16[16,64,768]{2,1,0:T(8,128)(2,1)}, u32[]{:S(2)}, u32[]{:S(2)}) async-start(bf16[16,64,768]{2,1,0:T(8,128)(2,1)} %broadcast_in_dim.8), calls=%async_computation | async-start | bytes 3145728 | tf_op jit(solution)/shard_map/all_to_all | solution.py:87
  21.7 1.9 broadcast_multiply_fusion
  23.6 1.0 copy-done.1
  24.6 1.3 constant_dynamic-slice_fusion.2
  25.9 16.2 %all-to-all-done = bf16[16,64,768]{2,1,0:T(8,128)(2,1)} async-done(((bf16[16,64,768]{2,1,0:T(8,128)(2,1)}), bf16[16,64,768]{2,1,0:T(8,128)(2,1)}, u32[]{:S(2)}, u32[]{:S(2)}) %all-to-all-start) | async-done | bytes 1572896 | tf_op jit(solution)/shard_map/all_to_all | solution.py:87
  42.1 1.9 collective-permute-start
  44.0 1.7 fusion.15
  45.8 2.1 fusion.12
  48.0 2.1 fusion.4
  50.2 1.6 fusion.5
  52.5 14.6 %all-to-all-start.1 = ((bf16[16,48,256]{2,1,0:T(8,128)(2,1)}), bf16[16,48,256]{2,1,0:T(8,128)(2,1)}, u32[]{:S(2)}, u32[]{:S(2)}) async-start(bf16[16,48,256]{2,1,0:T(8,128)(2,1)} %pad_maximum_fusion.3), calls=%async_computation.1 | async-start | bytes 786432 | tf_op jit(solution)/shard_map/all_to_all | solution.py:111
  67.1 16.8 %all-gather.3.cloned.1.call-done = bf16[2048,1536]{1,0:T(8,128)(2,1)} async-done(((bf16[64,1536]{1,0:T(8,128)(2,1)}), bf16[2048,1536]{1,0:T(8,128)(2,1)}) %all-gather.3.cloned.1.call-update) | async-done | bytes 6291472 | tf_op jit(solution)/shard_map/all_gather | solution.py:76
  83.9 3.9 %fusion.2 = f32[576,256]{1,0:T(8,128)S(1)} fusion(bf16[2048,256]{1,0:T(8,128)(2,1)} %copy-done.1, bf16[2048,1536]{1,0:T(8,128)(2,1)} %all-gather.3.cloned.1.call-done), kind=kOutput, calls=%fused_computation.2 | convolution fusion | flops 603979776 | bytes 4259840 | tf_op jit(solution)/shard_map/dot_general | solution.py:73
  87.8 1.3 fusion
  90.1 2.4 %all-to-all-done.1 = bf16[16,48,256]{2,1,0:T(8,128)(2,1)} async-done(((bf16[16,48,256]{2,1,0:T(8,128)(2,1)}), bf16[16,48,256]{2,1,0:T(8,128)(2,1)}, u32[]{:S(2)}, u32[]{:S(2)}) %all-to-all-start.1) | async-done | bytes 393248 | tf_op jit(solution)/shard_map/all_to_all | solution.py:111
  92.5 1.9 collective-permute-start.1
  94.6 1.1 convert_reduce_fusion.1
  95.7 7.9 %collective-permute-done.1 = bf16[8,96,256]{2,1,0:T(8,128)(2,1)} collective-permute-done((bf16[8,96,256]{2,1,0:T(8,128)(2,1)}, bf16[8,96,256]{2,1,0:T(8,128)(2,1)}, u32[]{:S(2)}, u32[]{:S(2)}) %collective-permute-start.1) | collective-permute-done | bytes 393248 | tf_op jit(solution)/shard_map/ppermute | solution.py:69
  103.6 1.1 add_convert_fusion
  105.5 12.2 %all-to-all-start.2 = ((bf16[8,112,256]{2,1,0:T(8,128)(2,1)}), bf16[8,112,256]{2,1,0:T(8,128)(2,1)S(1)}, u32[]{:S(2)}, u32[]{:S(2)}) async-start(bf16[8,112,256]{2,1,0:T(8,128)(2,1)} %pad_maximum_fusion.2), calls=%async_computation.2 | async-start | bytes 917504 | tf_op jit(solution)/shard_map/all_to_all | solution.py:134
  117.8 27.1 %all-to-all-done.2 = bf16[8,112,256]{2,1,0:T(8,128)(2,1)S(1)} async-done(((bf16[8,112,256]{2,1,0:T(8,128)(2,1)}), bf16[8,112,256]{2,1,0:T(8,128)(2,1)S(1)}, u32[]{:S(2)}, u32[]{:S(2)}) %all-to-all-start.2) | async-done | bytes 458784 | tf_op jit(solution)/shard_map/all_to_all | solution.py:134
  146.2 5.9 %all-to-all-start.3 = ((f32[32,8,128]{2,1,0:T(8,128)}), f32[32,8,128]{2,1,0:T(8,128)S(1)}, u32[]{:S(2)}, u32[]{:S(2)}) async-start(f32[32,8,128]{2,1,0:T(8,128)} %copy.33), calls=%async_computation.3 | async-start | bytes 262144 | tf_op jit(solution)/shard_map/all_to_all | solution.py:150
  152.2 6.5 %all-to-all-done.3 = f32[32,8,128]{2,1,0:T(8,128)S(1)} async-done(((f32[32,8,128]{2,1,0:T(8,128)}), f32[32,8,128]{2,1,0:T(8,128)S(1)}, u32[]{:S(2)}, u32[]{:S(2)}) %all-to-all-start.3) | async-done | bytes 131104 | tf_op jit(solution)/shard_map/all_to_all | solution.py:150
  159.4 4.9 %all-to-all-start.4 = ((f32[32,8,128]{2,1,0:T(8,128)}), f32[32,8,128]{2,1,0:T(8,128)S(1)}, u32[]{:S(2)}, u32[]{:S(2)}) async-start(f32[32,8,128]{2,1,0:T(8,128)} %broadcast_in_dim.10), calls=%async_computation.4 | async-start | bytes 262144 | tf_op jit(solution)/shard_map/all_to_all | solution.py:151
  164.9 6.2 %all-to-all-done.4 = f32[32,8,128]{2,1,0:T(8,128)S(1)} async-done(((f32[32,8,128]{2,1,0:T(8,128)}), f32[32,8,128]{2,1,0:T(8,128)S(1)}, u32[]{:S(2)}, u32[]{:S(2)}) %all-to-all-start.4) | async-done | bytes 131104 | tf_op jit(solution)/shard_map/all_to_all | solution.py:151
  175.5 1.9 collective-permute-start.2
  178.0 6.4 %all-to-all-start.5 = ((bf16[16,16,128]{2,1,0:T(8,128)(2,1)}), bf16[16,16,128]{2,1,0:T(8,128)(2,1)S(1)}, u32[]{:S(2)}, u32[]{:S(2)}) async-start(bf16[16,16,128]{2,1,0:T(8,128)(2,1)} %broadcast_in_dim.11), calls=%async_computation.5 | async-start | bytes 131072 | tf_op jit(solution)/shard_map/all_to_all | solution.py:160
  184.5 36.1 %all-gather = bf16[3840,128]{1,0:T(8,128)(2,1)S(1)} all-gather(bf16[240,128]{1,0:T(8,128)(2,1)S(1)} %slice.117), channel_id=2, replica_groups=mesh['pair'=8,'side'=2,'place'=16,'core'=2] {'pair','side'}, dimensions={0}, use_global_device_ids=true | all-gather | bytes 1044480 | tf_op jit(solution)/shard_map/all_gather | solution.py:161
  220.6 1.5 select_bitcast_fusion.2
  222.0 2.0 pad_maximum_fusion.1
  (78 shorter events, 12.3 us)
Async XLA Ops:
  6.5 87.9 %copy-start = (f32[18,256,128]{2,1,0:T(8,128)S(1)}, f32[18,256,128]{2,1,0:T(8,128)}, u32[]{:S(2)}) copy-start(f32[18,256,128]{2,1,0:T(8,128)} %param.10) | copy-start | bytes 7077892
  6.5 77.3 %all-gather.3.cloned.1.call-start = ((), (), s32[]{:S(2)}) async-start(), calls=%async_computation.6 | async-start | bytes 6488064 | tf_op jit(solution)/shard_map/all_gather | solution.py:76
  11.0 31.1 %all-to-all-start = ((bf16[16,64,768]{2,1,0:T(8,128)(2,1)}), bf16[16,64,768]{2,1,0:T(8,128)(2,1)}, u32[]{:S(2)}, u32[]{:S(2)}) async-start(bf16[16,64,768]{2,1,0:T(8,128)(2,1)} %broadcast_in_dim.8), calls=%async_computation | async-start | bytes 3145728 | tf_op jit(solution)/shard_map/all_to_all | solution.py:87
  23.6 1.0 copy-start.1
  42.1 5.9 %collective-permute-start = (bf16[1024,768]{1,0:T(8,128)(2,1)}, bf16[1024,768]{1,0:T(8,128)(2,1)}, u32[]{:S(2)}, u32[]{:S(2)}) collective-permute-start(bf16[1024,768]{1,0:T(8,128)(2,1)} %bitcast.2), channel_id=1, source_target_pairs={{0,1},{1,0},{2,3},{3,2},{4,5},{5,4},{6,7},{7,6},{8,9},{9,8},{10,11... | collective-permute-start | bytes 4718600 | tf_op jit(solution)/shard_map/ppermute | solution.py:69
  44.0 1.7 copy-start.4
  45.8 2.2 copy-start.3
  47.9 2.2 copy-start.2
  52.5 40.0 %all-to-all-start.1 = ((bf16[16,48,256]{2,1,0:T(8,128)(2,1)}), bf16[16,48,256]{2,1,0:T(8,128)(2,1)}, u32[]{:S(2)}, u32[]{:S(2)}) async-start(bf16[16,48,256]{2,1,0:T(8,128)(2,1)} %pad_maximum_fusion.3), calls=%async_computation.1 | async-start | bytes 786432 | tf_op jit(solution)/shard_map/all_to_all | solution.py:111
  83.9 3.9 %copy-start.5 = (bf16[2048,1536]{1,0:T(8,128)(2,1)S(1)}, bf16[2048,1536]{1,0:T(8,128)(2,1)}, u32[]{:S(2)}) copy-start(bf16[2048,1536]{1,0:T(8,128)(2,1)} %all-gather.3.cloned.1.call-done) | copy-start | bytes 18874372
  92.5 11.0 %collective-permute-start.1 = (bf16[8,96,256]{2,1,0:T(8,128)(2,1)}, bf16[8,96,256]{2,1,0:T(8,128)(2,1)}, u32[]{:S(2)}, u32[]{:S(2)}) collective-permute-start(bf16[8,96,256]{2,1,0:T(8,128)(2,1)} %fusion.17), channel_id=1, source_target_pairs={{0,32},{32,0},{1,33},{33,1},{2,34},{34,2},{3,35},{35,3},{4,36},{36... | collective-permute-start | bytes 1179656 | tf_op jit(solution)/shard_map/ppermute | solution.py:69
  105.5 39.5 %all-to-all-start.2 = ((bf16[8,112,256]{2,1,0:T(8,128)(2,1)}), bf16[8,112,256]{2,1,0:T(8,128)(2,1)S(1)}, u32[]{:S(2)}, u32[]{:S(2)}) async-start(bf16[8,112,256]{2,1,0:T(8,128)(2,1)} %pad_maximum_fusion.2), calls=%async_computation.2 | async-start | bytes 917504 | tf_op jit(solution)/shard_map/all_to_all | solution.py:134
  146.2 12.6 %all-to-all-start.3 = ((f32[32,8,128]{2,1,0:T(8,128)}), f32[32,8,128]{2,1,0:T(8,128)S(1)}, u32[]{:S(2)}, u32[]{:S(2)}) async-start(f32[32,8,128]{2,1,0:T(8,128)} %copy.33), calls=%async_computation.3 | async-start | bytes 262144 | tf_op jit(solution)/shard_map/all_to_all | solution.py:150
  159.4 11.7 %all-to-all-start.4 = ((f32[32,8,128]{2,1,0:T(8,128)}), f32[32,8,128]{2,1,0:T(8,128)S(1)}, u32[]{:S(2)}, u32[]{:S(2)}) async-start(f32[32,8,128]{2,1,0:T(8,128)} %broadcast_in_dim.10), calls=%async_computation.4 | async-start | bytes 262144 | tf_op jit(solution)/shard_map/all_to_all | solution.py:151
  175.5 45.1 %collective-permute-start.2 = (bf16[256,128]{1,0:T(8,128)(2,1)S(1)}, bf16[256,128]{1,0:T(8,128)(2,1)}, u32[]{:S(2)}, u32[]{:S(2)}) collective-permute-start(bf16[256,128]{1,0:T(8,128)(2,1)S(1)} %fusion.10), channel_id=1, source_target_pairs={{0,32},{32,0},{1,33},{33,1},{2,34},{34,2},{3,35},{35,3},{4,36},{36... | collective-permute-start | bytes 196616 | tf_op jit(solution)/shard_map/ppermute | solution.py:69
  178.0 44.0 %all-to-all-start.5 = ((bf16[16,16,128]{2,1,0:T(8,128)(2,1)}), bf16[16,16,128]{2,1,0:T(8,128)(2,1)S(1)}, u32[]{:S(2)}, u32[]{:S(2)}) async-start(bf16[16,16,128]{2,1,0:T(8,128)(2,1)} %broadcast_in_dim.11), calls=%async_computation.5 | async-start | bytes 131072 | tf_op jit(solution)/shard_map/all_to_all | solution.py:160
Sparse Core Ops, SparseCore 0:
  10.5 73.3 all-gather.2

commit v4 on v3

--- a/solution.py
+++ b/solution.py
@@ -73,9 +73,13 @@
         return lax.dot_general(heads, rows, contract, preferred_element_type=jnp.float32)
 
     heads = jnp.concatenate([head_cotangents, attention_out], axis=1).reshape(own_tok, mat_count, head_size)
-    late_heads = lax.all_gather(
-        heads[:, :groups, EARLY:].reshape(own_tok, groups * late_width), ("place", "core"), axis=0, tiled=True
+    late_heads = heads[:, :groups, EARLY:].reshape(own_tok, pairs, 2, late_width)
+    late_heads = [late_heads[:, :, s].reshape(own_tok, pairs * late_width) for s in range(2)]
+    late_heads = jnp.concatenate(
+        [jnp.where(side == 0, late_heads[1], late_heads[0]), jnp.where(side == 0, late_heads[0], late_heads[1])],
+        axis=1,
     )
+    late_heads = lax.all_gather(late_heads, ("place", "core"), axis=0, tiled=True)
 
     early_own = jnp.concatenate(
         [
@@ -110,19 +114,17 @@
     )
     early = lax.all_to_all(early, ("pair", "side"), 0, 0, tiled=True)
 
-    cut = in_mats * late_width
-    late = jnp.concatenate(
-        [
-            product(late_heads[:, :cut], features * live_mask),
-            product(late_heads[:, cut:], out_cotangent * live_mask),
-        ],
-        axis=0,
-    ).reshape(pairs, 2, late_width, row_count)
-    keep = jnp.where(side == 0, late[:, 0], late[:, 1])
-    give = jnp.where(side == 0, late[:, 1], late[:, 0]).astype(jnp.bfloat16)
-    early, keep, give = lax.optimization_barrier((early, keep, give))
+    cut, whole = in_mats // 2 * late_width, pairs * late_width
+
+    def late_part(at):
+        part_in = product(late_heads[:, at : at + cut], features * live_mask)
+        part_out = product(late_heads[:, at + cut : at + whole], out_cotangent * live_mask)
+        return jnp.concatenate([part_in, part_out], axis=0)
+
+    give, keep = late_part(0).astype(jnp.bfloat16), late_part(whole)
+    early, give = lax.optimization_barrier((early, give))
     got = exchange(give, "side")
-    late = (keep + got.astype(jnp.float32)).astype(jnp.bfloat16)
+    late = (keep + got.astype(jnp.float32)).astype(jnp.bfloat16).reshape(pairs, late_width, row_count)
     early_sum = jnp.sum(early.astype(jnp.float32), axis=0)
 
     moment_main = lax.dynamic_index_in_dim(momentum, 2 * pair + side, 0, keepdims=False).T
@@ -160,6 +162,7 @@
     tails = lax.all_to_all(tail, ("pair", "side"), 0, 0, tiled=True)
     updates = lax.all_gather(update[:cut], ("pair", "side"), axis=0)
     last = jnp.stack([jnp.where(side == 0, here, there), jnp.where(side == 0, there, here)])
+    last = lax.optimization_barrier(last)
     return jnp.concatenate([jnp.concatenate([updates, tails], axis=1), last], axis=0)
 
 

time: 232 us -> 231 us (level)
  waiting for transfers between devices: 83.1 us -> 80.1 us
  matrix products: 16.3 us -> 18.7 us
    ppermute x3, waiting for transfers between devices: 7.86 us -> 5.02 us  [exchange(): return lax.ppermute(array, axis, [(0, 1), (1, 0)])]
    dot_general x6 -> x8, matrix products: 12.7 us -> 15 us  [product(): lax.dot_general(heads, rows, contract, preferred_element_type=jnp.float32)]
  transfers between devices with their start and end apart: 10 -> 10, of which waited for: 7 -> 7; matrix products, arithmetic and copies ran while one was open for 10% -> 11% of each run, Pallas kernels for 0% -> 0%
where the time goes in v4:
time: 231 us; the launch traced here: 230 us
  waiting for transfers between devices  80.1 us (35%)
  starting transfers between devices  61.3 us (27%)
  blocking collectives  36.1 us (16%)
  matrix products  18.7 us (8%)
  between operations  14.6 us (6%)
  other arithmetic  10.5 us (5%)
  local copies, waits for them, and re-layouts  8.48 us (4%)
    all_gather x1, blocking collectives, local(): updates = lax.all_gather(update[:cut], ('pair', 'side'), axis=0)  36.1 us
    all_to_all x1, waiting for transfers between devices, local(): late = lax.all_to_all(late, 'pair', 0, 0, tiled=True)  27.1 us
    all_gather x1, waiting for transfers between devices, local(): lax.all_gather(late_heads, ('place', 'core'), axis=0, tiled=True)  18.9 us
    all_to_all x1, waiting for transfers between devices, local(): lax.all_to_all(jnp.broadcast_to(early_own[None], (places,) + early_own.sh...  16 us
    dot_general x8, matrix products, product(): lax.dot_general(heads, rows, contract, preferred_element_type=jnp.float32)  15 us
    all_to_all x1, starting transfers between devices, local(): early = lax.all_to_all(early, ('pair', 'side'), 0, 0, tiled=True)  14.7 us
    all_to_all x1, starting transfers between devices, local(): late = lax.all_to_all(late, 'pair', 0, 0, tiled=True)  12.2 us
    all_to_all x1, starting transfers between devices, local(): lax.all_to_all(jnp.broadcast_to(early_own[None], (places,) + early_own.sh...  10 us
  transfers between devices with their start and end apart: 10, of which 7 were waited for; matrix products, arithmetic and copies ran while one was open for 11% of the time, Pallas kernels for 0%

profile of v4, /device:TPU:2, one launch (start us, length us, event | category | flops | bytes accessed | tf_op | source)
XLA Modules:
  0.0 229.7 jit_solution(6723845031773299785)
XLA Ops:
  6.5 1.1 pad_maximum_fusion.4
  10.1 1.4 broadcast_in_dim.8
  11.5 10.0 %all-to-all-start = ((bf16[16,64,768]{2,1,0:T(8,128)(2,1)}), bf16[16,64,768]{2,1,0:T(8,128)(2,1)}, u32[]{:S(2)}, u32[]{:S(2)}) async-start(bf16[16,64,768]{2,1,0:T(8,128)(2,1)} %broadcast_in_dim.8), calls=%async_computation | async-start | bytes 3145728 | tf_op jit(solution)/shard_map/all_to_all | solution.py:91
  22.2 1.9 broadcast_multiply_fusion
  24.1 1.0 copy-done.1
  25.0 1.3 constant_dynamic-slice_fusion.2
  26.4 16.0 %all-to-all-done = bf16[16,64,768]{2,1,0:T(8,128)(2,1)} async-done(((bf16[16,64,768]{2,1,0:T(8,128)(2,1)}), bf16[16,64,768]{2,1,0:T(8,128)(2,1)}, u32[]{:S(2)}, u32[]{:S(2)}) %all-to-all-start) | async-done | bytes 1572896 | tf_op jit(solution)/shard_map/all_to_all | solution.py:91
  42.4 2.0 collective-permute-start
  44.4 1.7 fusion.26
  46.1 2.1 fusion.22
  48.3 0.8 fusion.11
  49.7 0.8 pad_maximum_fusion.2
  50.5 14.7 %all-to-all-start.1 = ((bf16[16,48,256]{2,1,0:T(8,128)(2,1)}), bf16[16,48,256]{2,1,0:T(8,128)(2,1)}, u32[]{:S(2)}, u32[]{:S(2)}) async-start(bf16[16,48,256]{2,1,0:T(8,128)(2,1)} %pad_maximum_fusion.2), calls=%async_computation.1 | async-start | bytes 786432 | tf_op jit(solution)/shard_map/all_to_all | solution.py:115
  65.4 18.9 %all-gather.3.cloned.1.call-done = bf16[2048,1536]{1,0:T(8,128)(2,1)} async-done(((bf16[64,1536]{1,0:T(8,128)(2,1)}), bf16[2048,1536]{1,0:T(8,128)(2,1)}) %all-gather.3.cloned.1.call-update) | async-done | bytes 6291472 | tf_op jit(solution)/shard_map/all_gather | solution.py:82
  84.3 2.8 %fusion.13 = bf16[288,256]{1,0:T(8,128)(2,1)S(1)} fusion(bf16[2048,256]{1,0:T(8,128)(2,1)S(1)} %get-tuple-element.31, bf16[2048,1536]{1,0:T(8,128)(2,1)} %all-gather.3.cloned.1.call-done), kind=kOutput, calls=%fused_computation.14 | convolution fusion | flops 302063616 | bytes 2768896 | tf_op jit(solution)/shard_map/dot_general | solution.py:73
  87.1 2.4 %fusion.8 = bf16[480,256]{1,0:T(8,128)(2,1)S(1)} fusion(bf16[2048,256]{1,0:T(8,128)(2,1)S(1)} %copy-done.2, bf16[2048,1536]{1,0:T(8,128)(2,1)} %all-gather.3.cloned.1.call-done), kind=kOutput, calls=%fused_computation.9 | convolution fusion | flops 503439360 | bytes 3391488 | tf_op jit(solution)/shard_map/dot_general | solution.py:73
  90.7 1.1 convert_reduce_fusion.1
  91.8 3.1 %collective-permute-start.1 = (bf16[768,256]{1,0:T(8,128)(2,1)}, bf16[768,256]{1,0:T(8,128)(2,1)S(1)}, u32[]{:S(2)}, u32[]{:S(2)}) collective-permute-start(bf16[768,256]{1,0:T(8,128)(2,1)} %pad_maximum_fusion.3), channel_id=1, source_target_pairs={{0,32},{32,0},{1,33},{33,1},{2,34},{34,2},{3,35},{35,3},{4,36},{36... | collective-permute-start | bytes 1179656 | tf_op jit(solution)/shard_map/ppermute | solution.py:69
  94.9 2.5 %fusion.4 = f32[288,256]{1,0:T(8,128)S(1)} fusion(bf16[2048,256]{1,0:T(8,128)(2,1)S(1)} %get-tuple-element.31, bf16[2048,1536]{1,0:T(8,128)(2,1)} %all-gather.3.cloned.1.call-done), kind=kOutput, calls=%fused_computation.4 | convolution fusion | flops 301989888 | bytes 2916352 | tf_op jit(solution)/shard_map/dot_general | solution.py:73
  97.5 2.3 %fusion = f32[480,256]{1,0:T(8,128)S(1)} fusion(bf16[2048,256]{1,0:T(8,128)(2,1)S(1)} %copy-done.3, bf16[2048,1536]{1,0:T(8,128)(2,1)} %all-gather.3.cloned.1.call-done), kind=kOutput, calls=%fused_computation | convolution fusion | flops 503316480 | bytes 3637248 | tf_op jit(solution)/shard_map/dot_general | solution.py:73
  99.8 5.0 %collective-permute-done.1 = bf16[768,256]{1,0:T(8,128)(2,1)S(1)} collective-permute-done((bf16[768,256]{1,0:T(8,128)(2,1)}, bf16[768,256]{1,0:T(8,128)(2,1)S(1)}, u32[]{:S(2)}, u32[]{:S(2)}) %collective-permute-start.1) | collective-permute-done | bytes 393248 | tf_op jit(solution)/shard_map/ppermute | solution.py:69
  105.7 12.2 %all-to-all-start.2 = ((bf16[8,112,256]{2,1,0:T(8,128)(2,1)}), bf16[8,112,256]{2,1,0:T(8,128)(2,1)S(1)}, u32[]{:S(2)}, u32[]{:S(2)}) async-start(bf16[8,112,256]{2,1,0:T(8,128)(2,1)} %pad_maximum_fusion.1), calls=%async_computation.2 | async-start | bytes 917504 | tf_op jit(solution)/shard_map/all_to_all | solution.py:136
  118.0 27.1 %all-to-all-done.2 = bf16[8,112,256]{2,1,0:T(8,128)(2,1)S(1)} async-done(((bf16[8,112,256]{2,1,0:T(8,128)(2,1)}), bf16[8,112,256]{2,1,0:T(8,128)(2,1)S(1)}, u32[]{:S(2)}, u32[]{:S(2)}) %all-to-all-start.2) | async-done | bytes 458784 | tf_op jit(solution)/shard_map/all_to_all | solution.py:136
  146.3 6.0 %all-to-all-start.3 = ((f32[32,8,128]{2,1,0:T(8,128)}), f32[32,8,128]{2,1,0:T(8,128)S(1)}, u32[]{:S(2)}, u32[]{:S(2)}) async-start(f32[32,8,128]{2,1,0:T(8,128)} %copy.29), calls=%async_computation.3 | async-start | bytes 262144 | tf_op jit(solution)/shard_map/all_to_all | solution.py:152
  152.4 6.5 %all-to-all-done.3 = f32[32,8,128]{2,1,0:T(8,128)S(1)} async-done(((f32[32,8,128]{2,1,0:T(8,128)}), f32[32,8,128]{2,1,0:T(8,128)S(1)}, u32[]{:S(2)}, u32[]{:S(2)}) %all-to-all-start.3) | async-done | bytes 131104 | tf_op jit(solution)/shard_map/all_to_all | solution.py:152
  159.7 4.9 %all-to-all-start.4 = ((f32[32,8,128]{2,1,0:T(8,128)}), f32[32,8,128]{2,1,0:T(8,128)S(1)}, u32[]{:S(2)}, u32[]{:S(2)}) async-start(f32[32,8,128]{2,1,0:T(8,128)} %broadcast_in_dim.10), calls=%async_computation.4 | async-start | bytes 262144 | tf_op jit(solution)/shard_map/all_to_all | solution.py:153
  165.2 6.1 %all-to-all-done.4 = f32[32,8,128]{2,1,0:T(8,128)S(1)} async-done(((f32[32,8,128]{2,1,0:T(8,128)}), f32[32,8,128]{2,1,0:T(8,128)S(1)}, u32[]{:S(2)}, u32[]{:S(2)}) %all-to-all-start.4) | async-done | bytes 131104 | tf_op jit(solution)/shard_map/all_to_all | solution.py:153
  175.8 1.9 collective-permute-start.2
  178.3 6.4 %all-to-all-start.5 = ((bf16[16,16,128]{2,1,0:T(8,128)(2,1)}), bf16[16,16,128]{2,1,0:T(8,128)(2,1)S(1)}, u32[]{:S(2)}, u32[]{:S(2)}) async-start(bf16[16,16,128]{2,1,0:T(8,128)(2,1)} %broadcast_in_dim.11), calls=%async_computation.5 | async-start | bytes 131072 | tf_op jit(solution)/shard_map/all_to_all | solution.py:162
  184.8 36.1 %all-gather = bf16[3840,128]{1,0:T(8,128)(2,1)S(1)} all-gather(bf16[240,128]{1,0:T(8,128)(2,1)S(1)} %slice.125), channel_id=2, replica_groups=mesh['pair'=8,'side'=2,'place'=16,'core'=2] {'pair','side'}, dimensions={0}, use_global_device_ids=true | all-gather | bytes 1044480 | tf_op jit(solution)/shard_map/all_gather | solution.py:163
  220.9 0.9 select_bitcast_fusion.1
  221.7 1.1 pad_maximum_fusion
  (85 shorter events, 12.8 us)
Async XLA Ops:
  6.5 58.7 %copy-start = (f32[18,256,128]{2,1,0:T(8,128)S(1)}, f32[18,256,128]{2,1,0:T(8,128)}, u32[]{:S(2)}) copy-start(f32[18,256,128]{2,1,0:T(8,128)} %param.10) | copy-start | bytes 7077892
  6.5 77.8 %all-gather.3.cloned.1.call-start = ((), (), s32[]{:S(2)}) async-start(), calls=%async_computation.6 | async-start | bytes 6488064 | tf_op jit(solution)/shard_map/all_gather | solution.py:82
  11.5 30.9 %all-to-all-start = ((bf16[16,64,768]{2,1,0:T(8,128)(2,1)}), bf16[16,64,768]{2,1,0:T(8,128)(2,1)}, u32[]{:S(2)}, u32[]{:S(2)}) async-start(bf16[16,64,768]{2,1,0:T(8,128)(2,1)} %broadcast_in_dim.8), calls=%async_computation | async-start | bytes 3145728 | tf_op jit(solution)/shard_map/all_to_all | solution.py:91
  24.1 1.0 copy-start.1
  42.4 3.7 %copy-start.6 = (bf16[16,1,64,256]{3,2,1,0:T(8,128)(2,1)S(1)}, bf16[16,1,64,256]{3,2,1,0:T(8,128)(2,1)}, u32[]{:S(2)}) copy-start(bf16[16,1,64,256]{3,2,1,0:T(8,128)(2,1)} %get-tuple-element.22) | copy-start | bytes 1572868
  42.4 5.9 %copy-start.5 = (bf16[16,1,64,256]{3,2,1,0:T(8,128)(2,1)S(1)}, bf16[16,1,64,256]{3,2,1,0:T(8,128)(2,1)}, u32[]{:S(2)}) copy-start(bf16[16,1,64,256]{3,2,1,0:T(8,128)(2,1)} %get-tuple-element.21) | copy-start | bytes 1572868
  42.4 5.8 %collective-permute-start = (bf16[1024,768]{1,0:T(8,128)(2,1)}, bf16[1024,768]{1,0:T(8,128)(2,1)S(1)}, u32[]{:S(2)}, u32[]{:S(2)}) collective-permute-start(bf16[1024,768]{1,0:T(8,128)(2,1)} %bitcast.2), channel_id=1, source_target_pairs={{0,1},{1,0},{2,3},{3,2},{4,5},{5,4},{6,7},{7,6},{8,9},{9,8},{10,11... | collective-permute-start | bytes 4718600 | tf_op jit(solution)/shard_map/ppermute | solution.py:69
  48.2 1.0 copy-start.4
  50.5 40.1 %all-to-all-start.1 = ((bf16[16,48,256]{2,1,0:T(8,128)(2,1)}), bf16[16,48,256]{2,1,0:T(8,128)(2,1)}, u32[]{:S(2)}, u32[]{:S(2)}) async-start(bf16[16,48,256]{2,1,0:T(8,128)(2,1)} %pad_maximum_fusion.2), calls=%async_computation.1 | async-start | bytes 786432 | tf_op jit(solution)/shard_map/all_to_all | solution.py:115
  84.3 2.8 %copy-start.2 = (bf16[2048,256]{1,0:T(8,128)(2,1)S(1)}, bf16[2048,256]{1,0:T(8,128)(2,1)}, u32[]{:S(2)}) copy-start(bf16[2048,256]{1,0:T(8,128)(2,1)} %copy-done.1) | copy-start | bytes 3145732
  90.7 6.8 %copy-start.3 = (bf16[2048,256]{1,0:T(8,128)(2,1)S(1)}, bf16[2048,256]{1,0:T(8,128)(2,1)}, u32[]{:S(2)}) copy-start(bf16[2048,256]{1,0:T(8,128)(2,1)} %copy-done.1) | copy-start | bytes 3145732
  91.8 13.0 %collective-permute-start.1 = (bf16[768,256]{1,0:T(8,128)(2,1)}, bf16[768,256]{1,0:T(8,128)(2,1)S(1)}, u32[]{:S(2)}, u32[]{:S(2)}) collective-permute-start(bf16[768,256]{1,0:T(8,128)(2,1)} %pad_maximum_fusion.3), channel_id=1, source_target_pairs={{0,32},{32,0},{1,33},{33,1},{2,34},{34,2},{3,35},{35,3},{4,36},{36... | collective-permute-start | bytes 1179656 | tf_op jit(solution)/shard_map/ppermute | solution.py:69
  105.7 39.4 %all-to-all-start.2 = ((bf16[8,112,256]{2,1,0:T(8,128)(2,1)}), bf16[8,112,256]{2,1,0:T(8,128)(2,1)S(1)}, u32[]{:S(2)}, u32[]{:S(2)}) async-start(bf16[8,112,256]{2,1,0:T(8,128)(2,1)} %pad_maximum_fusion.1), calls=%async_computation.2 | async-start | bytes 917504 | tf_op jit(solution)/shard_map/all_to_all | solution.py:136
  146.3 12.6 %all-to-all-start.3 = ((f32[32,8,128]{2,1,0:T(8,128)}), f32[32,8,128]{2,1,0:T(8,128)S(1)}, u32[]{:S(2)}, u32[]{:S(2)}) async-start(f32[32,8,128]{2,1,0:T(8,128)} %copy.29), calls=%async_computation.3 | async-start | bytes 262144 | tf_op jit(solution)/shard_map/all_to_all | solution.py:152
  159.7 11.7 %all-to-all-start.4 = ((f32[32,8,128]{2,1,0:T(8,128)}), f32[32,8,128]{2,1,0:T(8,128)S(1)}, u32[]{:S(2)}, u32[]{:S(2)}) async-start(f32[32,8,128]{2,1,0:T(8,128)} %broadcast_in_dim.10), calls=%async_computation.4 | async-start | bytes 262144 | tf_op jit(solution)/shard_map/all_to_all | solution.py:153
  175.8 45.1 %collective-permute-start.2 = (bf16[256,128]{1,0:T(8,128)(2,1)S(1)}, bf16[256,128]{1,0:T(8,128)(2,1)}, u32[]{:S(2)}, u32[]{:S(2)}) collective-permute-start(bf16[256,128]{1,0:T(8,128)(2,1)S(1)} %fusion.20), channel_id=1, source_target_pairs={{0,32},{32,0},{1,33},{33,1},{2,34},{34,2},{3,35},{35,3},{4,36},{36... | collective-permute-start | bytes 196616 | tf_op jit(solution)/shard_map/ppermute | solution.py:69
  178.3 43.4 %all-to-all-start.5 = ((bf16[16,16,128]{2,1,0:T(8,128)(2,1)}), bf16[16,16,128]{2,1,0:T(8,128)(2,1)S(1)}, u32[]{:S(2)}, u32[]{:S(2)}) async-start(bf16[16,16,128]{2,1,0:T(8,128)(2,1)} %broadcast_in_dim.11), calls=%async_computation.5 | async-start | bytes 131072 | tf_op jit(solution)/shard_map/all_to_all | solution.py:162
Sparse Core Ops, SparseCore 0:
  10.5 73.8 all-gather.2

commit v5 on v4

--- a/solution.py
+++ b/solution.py
@@ -122,7 +122,7 @@
         return jnp.concatenate([part_in, part_out], axis=0)
 
     give, keep = late_part(0).astype(jnp.bfloat16), late_part(whole)
-    early, give = lax.optimization_barrier((early, give))
+    early, keep = lax.optimization_barrier((early, keep))
     got = exchange(give, "side")
     late = (keep + got.astype(jnp.float32)).astype(jnp.bfloat16).reshape(pairs, late_width, row_count)
     early_sum = jnp.sum(early.astype(jnp.float32), axis=0)

time: 231 us -> 241 us (1.043)
  waiting for transfers between devices: 80.1 us -> 92.3 us
    all_to_all x1, waiting for transfers between devices: 0.01 us -> 12.8 us  [local(): tails = lax.all_to_all(tail, ('pair', 'side'), 0, 0, tiled=True)]
  transfers between devices with their start and end apart: 10 -> 10, of which waited for: 7 -> 7; matrix products, arithmetic and copies ran while one was open for 11% -> 10% of each run, Pallas kernels for 0% -> 0%
where the time goes in v5:
time: 241 us; the launch traced here: 240 us
  waiting for transfers between devices  92.3 us (38%)
  starting transfers between devices  61.1 us (25%)
  blocking collectives  35 us (15%)
  matrix products  18.4 us (8%)
  between operations  14.6 us (6%)
  other arithmetic  10.6 us (4%)
  local copies, waits for them, and re-layouts  8.36 us (3%)
    all_gather x1, blocking collectives, local(): updates = lax.all_gather(update[:cut], ('pair', 'side'), axis=0)  35 us
    all_to_all x1, waiting for transfers between devices, local(): late = lax.all_to_all(late, 'pair', 0, 0, tiled=True)  27.3 us
    all_gather x1, waiting for transfers between devices, local(): lax.all_gather(late_heads, ('place', 'core'), axis=0, tiled=True)  16.6 us
    all_to_all x1, waiting for transfers between devices, local(): lax.all_to_all(jnp.broadcast_to(early_own[None], (places,) + early_own.sh...  16 us
    dot_general x8, matrix products, product(): lax.dot_general(heads, rows, contract, preferred_element_type=jnp.float32)  14.8 us
    all_to_all x1, starting transfers between devices, local(): early = lax.all_to_all(early, ('pair', 'side'), 0, 0, tiled=True)  14.7 us
    all_to_all x1, waiting for transfers between devices, local(): tails = lax.all_to_all(tail, ('pair', 'side'), 0, 0, tiled=True)  12.8 us
    all_to_all x1, starting transfers between devices, local(): late = lax.all_to_all(late, 'pair', 0, 0, tiled=True)  12.2 us
  transfers between devices with their start and end apart: 10, of which 7 were waited for; matrix products, arithmetic and copies ran while one was open for 10% of the time, Pallas kernels for 0%

profile of v5, /device:TPU:2, one launch (start us, length us, event | category | flops | bytes accessed | tf_op | source)
XLA Modules:
  0.0 240.5 jit_solution(1018812588428596991)
XLA Ops:
  6.5 1.1 pad_maximum_fusion.5
  10.1 1.4 broadcast_in_dim.8
  11.5 10.0 %all-to-all-start = ((bf16[16,64,768]{2,1,0:T(8,128)(2,1)}), bf16[16,64,768]{2,1,0:T(8,128)(2,1)}, u32[]{:S(2)}, u32[]{:S(2)}) async-start(bf16[16,64,768]{2,1,0:T(8,128)(2,1)} %broadcast_in_dim.8), calls=%async_computation | async-start | bytes 3145728 | tf_op jit(solution)/shard_map/all_to_all | solution.py:91
  22.2 1.9 broadcast_multiply_fusion
  24.1 1.0 copy-done.1
  25.0 1.4 constant_dynamic-slice_fusion.2
  26.4 16.0 %all-to-all-done = bf16[16,64,768]{2,1,0:T(8,128)(2,1)} async-done(((bf16[16,64,768]{2,1,0:T(8,128)(2,1)}), bf16[16,64,768]{2,1,0:T(8,128)(2,1)}, u32[]{:S(2)}, u32[]{:S(2)}) %all-to-all-start) | async-done | bytes 1572896 | tf_op jit(solution)/shard_map/all_to_all | solution.py:91
  42.4 1.9 collective-permute-start
  44.5 1.7 fusion.25
  46.2 2.2 fusion.22
  48.5 2.1 fusion.11
  50.7 1.6 fusion.12
  53.1 14.7 %all-to-all-start.1 = ((bf16[16,48,256]{2,1,0:T(8,128)(2,1)}), bf16[16,48,256]{2,1,0:T(8,128)(2,1)}, u32[]{:S(2)}, u32[]{:S(2)}) async-start(bf16[16,48,256]{2,1,0:T(8,128)(2,1)} %pad_maximum_fusion.3), calls=%async_computation.1 | async-start | bytes 786432 | tf_op jit(solution)/shard_map/all_to_all | solution.py:115
  67.7 16.6 %all-gather.3.cloned.1.call-done = bf16[2048,1536]{1,0:T(8,128)(2,1)} async-done(((bf16[64,1536]{1,0:T(8,128)(2,1)}), bf16[2048,1536]{1,0:T(8,128)(2,1)}) %all-gather.3.cloned.1.call-update) | async-done | bytes 6291472 | tf_op jit(solution)/shard_map/all_gather | solution.py:82
  84.3 2.8 %fusion.13 = bf16[288,256]{1,0:T(8,128)(2,1)S(1)} fusion(bf16[2048,256]{1,0:T(8,128)(2,1)S(1)} %get-tuple-element.31, bf16[2048,1536]{1,0:T(8,128)(2,1)} %all-gather.3.cloned.1.call-done), kind=kOutput, calls=%fused_computation.14 | convolution fusion | flops 302063616 | bytes 2768896 | tf_op jit(solution)/shard_map/dot_general | solution.py:73
  87.1 2.5 %fusion.8 = bf16[480,256]{1,0:T(8,128)(2,1)S(1)} fusion(bf16[2048,256]{1,0:T(8,128)(2,1)S(1)} %copy-done.2, bf16[2048,1536]{1,0:T(8,128)(2,1)} %all-gather.3.cloned.1.call-done), kind=kOutput, calls=%fused_computation.9 | convolution fusion | flops 503439360 | bytes 3391488 | tf_op jit(solution)/shard_map/dot_general | solution.py:73
  90.4 3.4 %collective-permute-start.1 = (bf16[768,256]{1,0:T(8,128)(2,1)}, bf16[768,256]{1,0:T(8,128)(2,1)}, u32[]{:S(2)}, u32[]{:S(2)}) collective-permute-start(bf16[768,256]{1,0:T(8,128)(2,1)} %pad_maximum_fusion.4), channel_id=1, source_target_pairs={{0,32},{32,0},{1,33},{33,1},{2,34},{34,2},{3,35},{35,3},{4,36},{36... | collective-permute-start | bytes 1179656 | tf_op jit(solution)/shard_map/ppermute | solution.py:69
  93.9 1.1 fusion.6
  95.8 1.1 convert_reduce_fusion.1
  96.9 7.0 %collective-permute-done.1 = bf16[768,256]{1,0:T(8,128)(2,1)} collective-permute-done((bf16[768,256]{1,0:T(8,128)(2,1)}, bf16[768,256]{1,0:T(8,128)(2,1)}, u32[]{:S(2)}, u32[]{:S(2)}) %collective-permute-start.1) | collective-permute-done | bytes 393248 | tf_op jit(solution)/shard_map/ppermute | solution.py:69
  103.9 1.1 add_convert_fusion
  105.8 12.2 %all-to-all-start.2 = ((bf16[8,112,256]{2,1,0:T(8,128)(2,1)}), bf16[8,112,256]{2,1,0:T(8,128)(2,1)S(1)}, u32[]{:S(2)}, u32[]{:S(2)}) async-start(bf16[8,112,256]{2,1,0:T(8,128)(2,1)} %pad_maximum_fusion.2), calls=%async_computation.2 | async-start | bytes 917504 | tf_op jit(solution)/shard_map/all_to_all | solution.py:136
  118.1 27.3 %all-to-all-done.2 = bf16[8,112,256]{2,1,0:T(8,128)(2,1)S(1)} async-done(((bf16[8,112,256]{2,1,0:T(8,128)(2,1)}), bf16[8,112,256]{2,1,0:T(8,128)(2,1)S(1)}, u32[]{:S(2)}, u32[]{:S(2)}) %all-to-all-start.2) | async-done | bytes 458784 | tf_op jit(solution)/shard_map/all_to_all | solution.py:136
  146.7 5.7 %all-to-all-start.3 = ((f32[32,8,128]{2,1,0:T(8,128)}), f32[32,8,128]{2,1,0:T(8,128)S(1)}, u32[]{:S(2)}, u32[]{:S(2)}) async-start(f32[32,8,128]{2,1,0:T(8,128)} %copy.29), calls=%async_computation.3 | async-start | bytes 262144 | tf_op jit(solution)/shard_map/all_to_all | solution.py:152
  152.5 6.5 %all-to-all-done.3 = f32[32,8,128]{2,1,0:T(8,128)S(1)} async-done(((f32[32,8,128]{2,1,0:T(8,128)}), f32[32,8,128]{2,1,0:T(8,128)S(1)}, u32[]{:S(2)}, u32[]{:S(2)}) %all-to-all-start.3) | async-done | bytes 131104 | tf_op jit(solution)/shard_map/all_to_all | solution.py:152
  159.8 4.9 %all-to-all-start.4 = ((f32[32,8,128]{2,1,0:T(8,128)}), f32[32,8,128]{2,1,0:T(8,128)S(1)}, u32[]{:S(2)}, u32[]{:S(2)}) async-start(f32[32,8,128]{2,1,0:T(8,128)} %broadcast_in_dim.10), calls=%async_computation.4 | async-start | bytes 262144 | tf_op jit(solution)/shard_map/all_to_all | solution.py:153
  165.3 6.1 %all-to-all-done.4 = f32[32,8,128]{2,1,0:T(8,128)S(1)} async-done(((f32[32,8,128]{2,1,0:T(8,128)}), f32[32,8,128]{2,1,0:T(8,128)S(1)}, u32[]{:S(2)}, u32[]{:S(2)}) %all-to-all-start.4) | async-done | bytes 131104 | tf_op jit(solution)/shard_map/all_to_all | solution.py:153
  175.8 1.9 collective-permute-start.2
  177.8 35.0 %all-gather = bf16[3840,128]{1,0:T(8,128)(2,1)S(1)} all-gather(bf16[240,128]{1,0:T(8,128)(2,1)S(1)} %slice.125), channel_id=2, replica_groups=mesh['pair'=8,'side'=2,'place'=16,'core'=2] {'pair','side'}, dimensions={0}, use_global_device_ids=true | all-gather | bytes 1044480 | tf_op jit(solution)/shard_map/all_gather | solution.py:163
  213.4 6.3 %all-to-all-start.5 = ((bf16[16,16,128]{2,1,0:T(8,128)(2,1)}), bf16[16,16,128]{2,1,0:T(8,128)(2,1)S(1)}, u32[]{:S(2)}, u32[]{:S(2)}) async-start(bf16[16,16,128]{2,1,0:T(8,128)(2,1)} %broadcast_in_dim.11), calls=%async_computation.5 | async-start | bytes 131072 | tf_op jit(solution)/shard_map/all_to_all | solution.py:162
  219.7 12.8 %all-to-all-done.5 = bf16[16,16,128]{2,1,0:T(8,128)(2,1)S(1)} async-done(((bf16[16,16,128]{2,1,0:T(8,128)(2,1)}), bf16[16,16,128]{2,1,0:T(8,128)(2,1)S(1)}, u32[]{:S(2)}, u32[]{:S(2)}) %all-to-all-start.5) | async-done | bytes 65568 | tf_op jit(solution)/shard_map/all_to_all | solution.py:162
  232.5 1.1 pad_maximum_fusion
  (84 shorter events, 13.4 us)
Async XLA Ops:
  6.5 37.8 %copy-start = (f32[18,256,128]{2,1,0:T(8,128)S(1)}, f32[18,256,128]{2,1,0:T(8,128)}, u32[]{:S(2)}) copy-start(f32[18,256,128]{2,1,0:T(8,128)} %param.10) | copy-start | bytes 7077892
  6.5 77.8 %all-gather.3.cloned.1.call-start = ((), (), s32[]{:S(2)}) async-start(), calls=%async_computation.6 | async-start | bytes 6488064 | tf_op jit(solution)/shard_map/all_gather | solution.py:82
  11.5 30.9 %all-to-all-start = ((bf16[16,64,768]{2,1,0:T(8,128)(2,1)}), bf16[16,64,768]{2,1,0:T(8,128)(2,1)}, u32[]{:S(2)}, u32[]{:S(2)}) async-start(bf16[16,64,768]{2,1,0:T(8,128)(2,1)} %broadcast_in_dim.8), calls=%async_computation | async-start | bytes 3145728 | tf_op jit(solution)/shard_map/all_to_all | solution.py:91
  24.1 1.0 copy-start.1
  42.4 6.1 %collective-permute-start = (bf16[1024,768]{1,0:T(8,128)(2,1)}, bf16[1024,768]{1,0:T(8,128)(2,1)}, u32[]{:S(2)}, u32[]{:S(2)}) collective-permute-start(bf16[1024,768]{1,0:T(8,128)(2,1)} %bitcast.2), channel_id=1, source_target_pairs={{0,1},{1,0},{2,3},{3,2},{4,5},{5,4},{6,7},{7,6},{8,9},{9,8},{10,11... | collective-permute-start | bytes 4718600 | tf_op jit(solution)/shard_map/ppermute | solution.py:69
  44.5 4.0 %copy-start.4 = (bf16[16,1,64,256]{3,2,1,0:T(8,128)(2,1)S(1)}, bf16[16,1,64,256]{3,2,1,0:T(8,128)(2,1)}, u32[]{:S(2)}) copy-start(bf16[16,1,64,256]{3,2,1,0:T(8,128)(2,1)} %get-tuple-element.21) | copy-start | bytes 1572868
  48.5 2.2 copy-start.3
  53.1 42.8 %all-to-all-start.1 = ((bf16[16,48,256]{2,1,0:T(8,128)(2,1)}), bf16[16,48,256]{2,1,0:T(8,128)(2,1)}, u32[]{:S(2)}, u32[]{:S(2)}) async-start(bf16[16,48,256]{2,1,0:T(8,128)(2,1)} %pad_maximum_fusion.3), calls=%async_computation.1 | async-start | bytes 786432 | tf_op jit(solution)/shard_map/all_to_all | solution.py:115
  84.3 2.8 %copy-start.2 = (bf16[2048,256]{1,0:T(8,128)(2,1)S(1)}, bf16[2048,256]{1,0:T(8,128)(2,1)}, u32[]{:S(2)}) copy-start(bf16[2048,256]{1,0:T(8,128)(2,1)} %copy-done.1) | copy-start | bytes 3145732
  87.1 6.8 %copy-start.5 = (bf16[2048,1536]{1,0:T(8,128)(2,1)S(1)}, bf16[2048,1536]{1,0:T(8,128)(2,1)}, u32[]{:S(2)}) copy-start(bf16[2048,1536]{1,0:T(8,128)(2,1)} %all-gather.3.cloned.1.call-done) | copy-start | bytes 18874372
  90.4 13.5 %collective-permute-start.1 = (bf16[768,256]{1,0:T(8,128)(2,1)}, bf16[768,256]{1,0:T(8,128)(2,1)}, u32[]{:S(2)}, u32[]{:S(2)}) collective-permute-start(bf16[768,256]{1,0:T(8,128)(2,1)} %pad_maximum_fusion.4), channel_id=1, source_target_pairs={{0,32},{32,0},{1,33},{33,1},{2,34},{34,2},{3,35},{35,3},{4,36},{36... | collective-permute-start | bytes 1179656 | tf_op jit(solution)/shard_map/ppermute | solution.py:69
  105.8 39.7 %all-to-all-start.2 = ((bf16[8,112,256]{2,1,0:T(8,128)(2,1)}), bf16[8,112,256]{2,1,0:T(8,128)(2,1)S(1)}, u32[]{:S(2)}, u32[]{:S(2)}) async-start(bf16[8,112,256]{2,1,0:T(8,128)(2,1)} %pad_maximum_fusion.2), calls=%async_computation.2 | async-start | bytes 917504 | tf_op jit(solution)/shard_map/all_to_all | solution.py:136
  146.7 12.4 %all-to-all-start.3 = ((f32[32,8,128]{2,1,0:T(8,128)}), f32[32,8,128]{2,1,0:T(8,128)S(1)}, u32[]{:S(2)}, u32[]{:S(2)}) async-start(f32[32,8,128]{2,1,0:T(8,128)} %copy.29), calls=%async_computation.3 | async-start | bytes 262144 | tf_op jit(solution)/shard_map/all_to_all | solution.py:152
  159.8 11.7 %all-to-all-start.4 = ((f32[32,8,128]{2,1,0:T(8,128)}), f32[32,8,128]{2,1,0:T(8,128)S(1)}, u32[]{:S(2)}, u32[]{:S(2)}) async-start(f32[32,8,128]{2,1,0:T(8,128)} %broadcast_in_dim.10), calls=%async_computation.4 | async-start | bytes 262144 | tf_op jit(solution)/shard_map/all_to_all | solution.py:153
  175.8 43.8 %collective-permute-start.2 = (bf16[256,128]{1,0:T(8,128)(2,1)S(1)}, bf16[256,128]{1,0:T(8,128)(2,1)S(1)}, u32[]{:S(2)}, u32[]{:S(2)}) collective-permute-start(bf16[256,128]{1,0:T(8,128)(2,1)S(1)} %fusion.20), channel_id=1, source_target_pairs={{0,32},{32,0},{1,33},{33,1},{2,34},{34,2},{3,35},{35,3},{4,36},{36... | collective-permute-start | bytes 196616 | tf_op jit(solution)/shard_map/ppermute | solution.py:69
  213.4 19.1 %all-to-all-start.5 = ((bf16[16,16,128]{2,1,0:T(8,128)(2,1)}), bf16[16,16,128]{2,1,0:T(8,128)(2,1)S(1)}, u32[]{:S(2)}, u32[]{:S(2)}) async-start(bf16[16,16,128]{2,1,0:T(8,128)(2,1)} %broadcast_in_dim.11), calls=%async_computation.5 | async-start | bytes 131072 | tf_op jit(solution)/shard_map/all_to_all | solution.py:162
Sparse Core Ops, SparseCore 0:
  10.5 73.7 all-gather.2
